TPU v7x, 128 devices: a whole 4x4x4 slice. The times are simulated.
128 devices in a mesh: hst: 16 (over y, z), chip: 8 (over x, core).
Axes of the slice: x: 4, y: 4, z: 4, core: 2. Of those that a mesh axis runs over, the one named last changes fastest.
Arguments:
- dense_feats: bfloat16 [32768, 13], P(('hst', 'chip')), may hold values from -6 to 6
- labels: int32 [32768], P(('hst', 'chip')), may hold values 0 or 1
- slot_ids: int32 [32768, 26], P(('hst', 'chip')), may hold values from 0 to 2047
- needed_owner: int32 [262144, 1], P(('hst', 'chip')), may hold values from 0 to 127; in each aligned block of 2048 rows (0 to 2047, 2048 to 4095, ...) at most 32 rows name the same one
- needed_local: int32 [262144], P(('hst', 'chip')), may hold values from 0 to 4095
- evicted: int32 [262144], P(('hst', 'chip')), may hold values 0 or 1
- table_rows: bfloat16 [524288, 128], P(('hst', 'chip')), may hold values from -4 to 4
- table_scale: float32 [524288], P(('hst', 'chip')), may hold values from 0.3 to 3
- table_acc: float32 [524288], P(('hst', 'chip')), may hold values from 0.0001 to 0.01
- cross_down: bfloat16 [3341, 512], replicated, may hold values from -0.109375 to 0.109375
- cross_up: bfloat16 [512, 3341], replicated, may hold values from -0.25 to 0.25
- cross_bias: float32 [3341], replicated, may hold values from -3 to 3
- hidden_weight: bfloat16 [3341, 512], replicated, may hold values from -0.109375 to 0.109375
- hidden_bias: float32 [512], replicated, may hold values from -3 to 3
- out_weight: bfloat16 [512], replicated, may hold values from -0.25 to 0.25
Outputs:
- new_rows: bfloat16 [524288, 128], P(('hst', 'chip'))
- new_scale: float32 [524288], P(('hst', 'chip'))
- new_accum: float32 [524288], P(('hst', 'chip'))
- cache_grad: float32 [262144, 128], P(('hst', 'chip'))
- grad_cross_in: float32 [512, 3341], P(('hst', 'chip'))
- grad_hidden_in: float32 [512, 3341], P(('hst', 'chip'))
- grad_cross_out: float32 [512, 3341], P(('hst', 'chip'))
Inputs may be any that keep to these rules, and one draw needn't show every extreme that they name: `needed_owner`: among the 2048 slots of one device at most 32 name the same owner, and in every draw some owner is named exactly 32 times by some device.
All inputs are finite; a program needn't handle non-finite values. No bound on the sum of `labels` or of `evicted` on one device may be relied on, other than what follows from the above.
Results may differ from a plain program's by a relative error of at most 0.0099.
Values may be sent and summed in bfloat16 or wider, within the bound.
A program may use at most 192 MiB of HBM per device.

v0:
```python
import jax
import jax.numpy as jnp
from jax import lax
from jax.sharding import PartitionSpec as P

LEARN_RATE = 0.1
QUANT_TOP = 4.0


def contract_last(left, right):
    return lax.dot_general(
        left, right, (((1,), (1,)), ((), ())), preferred_element_type=jnp.float32
    )


def contract_first(left, right):
    return lax.dot_general(
        left, right, (((0,), (0,)), ((), ())), preferred_element_type=jnp.float32
    )


def send_requests(requests):
    return lax.all_to_all(requests, ("hst", "chip"), split_axis=0, concat_axis=0, tiled=True)


def send_values(served):
    return lax.all_to_all(served, ("hst", "chip"), split_axis=0, concat_axis=0, tiled=True)


def send_grads(outgoing):
    return lax.all_to_all(outgoing, ("hst", "chip"), split_axis=0, concat_axis=0, tiled=True)


def dense_step(
    base_in, labels, cross_down, cross_up, cross_bias, hidden_weight, hidden_bias, out_weight
):
    low_rank = jnp.dot(base_in, cross_down, preferred_element_type=jnp.float32).astype(jnp.bfloat16)
    mixing = jnp.dot(low_rank, cross_up, preferred_element_type=jnp.float32)
    base_wide = base_in.astype(jnp.float32)
    crossed = (base_wide * (mixing + cross_bias[None, :]) + base_wide).astype(jnp.bfloat16)
    preact = (
        jnp.dot(crossed, hidden_weight, preferred_element_type=jnp.float32) + hidden_bias[None, :]
    )
    sig_pre = jax.nn.sigmoid(preact)
    hidden = (preact * sig_pre).astype(jnp.bfloat16)
    logits = jnp.dot(hidden, out_weight, preferred_element_type=jnp.float32)
    grad_logit = jax.nn.sigmoid(logits) - labels.astype(jnp.float32)
    slope = sig_pre * (1.0 + preact * (1.0 - sig_pre))
    grad_hidden = (grad_logit[:, None] * out_weight.astype(jnp.float32)[None, :] * slope).astype(
        jnp.bfloat16
    )
    grad_cross = contract_last(grad_hidden, hidden_weight)
    grad_mix = (grad_cross * base_wide).astype(jnp.bfloat16)
    grad_low = contract_last(grad_mix, cross_up).astype(jnp.bfloat16)
    grad_input = grad_cross * (mixing + cross_bias[None, :] + 1.0) + contract_last(
        grad_low, cross_down
    )
    return (low_rank, crossed, grad_hidden, grad_mix, grad_low, grad_input)


def on_device(
    dense_feats,
    labels,
    slot_ids,
    needed_owner,
    needed_local,
    evicted,
    table_rows,
    table_scale,
    table_acc,
    cross_down,
    cross_up,
    cross_bias,
    hidden_weight,
    hidden_bias,
    out_weight,
):
    n_host = lax.axis_size("hst")
    n_chip = lax.axis_size("chip")
    devices = n_host * n_chip
    owners = needed_owner[:, 0]
    need_rows = owners.shape[0]
    capacity = 2 * need_rows // devices
    emb_width = table_rows.shape[1]
    batch_rows = dense_feats.shape[0]
    owner_hits = (owners[:, None] == jnp.arange(devices, dtype=jnp.int32)[None, :]).astype(
        jnp.int32
    )
    places = jnp.sum(jnp.cumsum(owner_hits, axis=0) * owner_hits, axis=1) - 1
    requests = jnp.full((devices, capacity), -1, jnp.int32).at[owners, places].set(needed_local)
    incoming = send_requests(requests)
    row_index = jnp.where(incoming >= 0, incoming, 0)
    served = (
        table_rows[row_index].astype(jnp.float32) * table_scale[row_index][:, :, None]
    ).astype(jnp.bfloat16)
    returned = send_values(served)
    fetched = returned[owners, places]
    embedded = fetched[slot_ids].reshape(batch_rows, -1)
    base_in = jnp.concatenate([embedded, dense_feats], axis=1)
    low_rank, crossed, grad_hidden, grad_mix, grad_low, grad_input = dense_step(
        base_in, labels, cross_down, cross_up, cross_bias, hidden_weight, hidden_bias, out_weight
    )
    emb_cols = embedded.shape[1]
    emb_grad = grad_input[:, :emb_cols].reshape(-1, emb_width)
    slot_grad = jax.ops.segment_sum(emb_grad, slot_ids.reshape(-1), num_segments=need_rows)
    evict_wide = evicted.astype(jnp.float32)[:, None]
    cache_grad = slot_grad * (1.0 - evict_wide)
    outgoing = (
        jnp.zeros((devices, capacity, emb_width), jnp.float32)
        .at[owners, places]
        .set(slot_grad * evict_wide)
    )
    received = send_grads(outgoing)
    row_grad = jax.ops.segment_sum(
        received.reshape(-1, emb_width), row_index.reshape(-1), num_segments=table_rows.shape[0]
    )
    new_accum = table_acc + jnp.mean(row_grad * row_grad, axis=1)
    values = (
        table_rows.astype(jnp.float32) * table_scale[:, None]
        - LEARN_RATE * row_grad / jnp.sqrt(new_accum)[:, None]
    )
    new_scale = (jnp.max(jnp.abs(values), axis=1) + 1e-06) / QUANT_TOP
    new_rows = (values / new_scale[:, None]).astype(jnp.bfloat16)
    partials = (
        contract_first(grad_low, base_in) / devices,
        contract_first(grad_hidden, crossed) / devices,
        contract_first(low_rank, grad_mix) / devices,
    )
    grad_down, grad_hid, grad_up = (
        lax.psum_scatter(partials[0], ("hst", "chip"), scatter_dimension=0, tiled=True),
        lax.psum_scatter(partials[1], ("hst", "chip"), scatter_dimension=0, tiled=True),
        lax.psum_scatter(partials[2], ("hst", "chip"), scatter_dimension=0, tiled=True),
    )
    return (new_rows, new_scale, new_accum, cache_grad, grad_down, grad_hid, grad_up)


def solution(mesh):
    placed = (
        P(("hst", "chip"), None),
        P(("hst", "chip")),
        P(("hst", "chip"), None),
        P(("hst", "chip"), None),
        P(("hst", "chip")),
        P(("hst", "chip")),
        P(("hst", "chip"), None),
        P(("hst", "chip")),
        P(("hst", "chip")),
        P(),
        P(),
        P(),
        P(),
        P(),
        P(),
    )
    return jax.shard_map(
        on_device,
        mesh=mesh,
        in_specs=placed,
        out_specs=(
            P(("hst", "chip"), None),
            P(("hst", "chip")),
            P(("hst", "chip")),
            P(("hst", "chip"), None),
            P(("hst", "chip"), None),
            P(("hst", "chip"), None),
            P(("hst", "chip"), None),
        ),
        check_vma=False,
    )
```

profile of v0, /device:TPU:6, one launch (start us, length us, event | category | flops | bytes accessed | tf_op | source)
XLA Modules:
  0.0 450.7 jit_solution(11062601567012717333)
XLA Ops:
  7.2 1.0 copy.40
  8.2 0.3 fusion.6
  8.5 1.0 copy-done.9
  9.5 1.3 broadcast_add_fusion
  10.8 0.3 copy.41
  11.2 0.6 fusion.3
  11.9 0.1 and_reduce_fusion
  12.0 0.1 multiply_reduce_fusion.1
  12.1 0.6 broadcast_select_fusion
  12.7 8.2 %scatter_custom_fusion.2 = s32[4096]{0:T(1024)S(1)} fusion(s32[2048]{0:T(1024)S(1)} %get-tuple-element.22, s32[2048]{0:T(1024)} %param.19, s32[]{:T(128)} %constant.14.clone.1), kind=kCustom, calls=%fused_computation.66 | custom fusion | bytes 16896
  21.0 0.7 copy.42
  21.7 18.7 %all_to_all.25 = s32[128,1,32]{2,1,0:T(1,128)S(1)} all-to-all(s32[128,1,32]{2,1,0:T(1,128)} %copy.42), channel_id=1, replica_groups=mesh['hst'=16,'chip'=8] {'hst','chip'}, dimensions={0} | all-to-all | bytes 32768 | tf_op jit(solution)/shard_map/all_to_all | solution.py:23
  40.4 0.6 compare_select_fusion
  41.1 0.9 reshape.136
  42.0 15.7 %gather_fusion = bf16[4096,128]{1,0:T(8,128)(2,1)} fusion(bf16[4096,128]{1,0:T(8,128)(2,1)} %param.21, s32[4096]{0:T(1024)S(1)} %broadcast_clamp_fusion), kind=kCustom, calls=%fused_computation | custom fusion | bytes 2113536 | tf_op jit(solution)/shard_map/gather | solution.py:94
  57.7 40.5 %gather_fusion.1 = f32[4096]{0:T(1024)} fusion(f32[4096]{0:T(1024)S(1)} %copy-done.2, s32[4096]{0:T(1024)S(1)} %broadcast_clamp_fusion), kind=kCustom, calls=%fused_computation.1 | custom fusion | bytes 49152 | tf_op jit(solution)/shard_map/gather | solution.py:94
  98.3 1.4 reshape.143
  99.7 2.5 fusion.2
  102.3 6.6 %all-to-all-start.1 = ((bf16[128,32,128]{2,1,0:T(8,128)(2,1)}), bf16[128,32,128]{2,1,0:T(8,128)(2,1)}, u32[]{:S(2)}, u32[]{:S(2)}) async-start(bf16[128,32,128]{2,1,0:T(8,128)(2,1)} %fusion.2), calls=%async_computation.1 | async-start | bytes 2097152 | tf_op jit(solution)/shard_map/all_to_all | solution.py:27
  108.9 1.4 compare_select_fusion.3
  110.3 1.5 copy.44
  111.8 1.6 reshape.158
  113.5 0.8 pad_clamp_fusion
  114.2 12.0 %all-to-all-done.1 = bf16[128,32,128]{2,1,0:T(8,128)(2,1)} async-done(((bf16[128,32,128]{2,1,0:T(8,128)(2,1)}), bf16[128,32,128]{2,1,0:T(8,128)(2,1)}, u32[]{:S(2)}, u32[]{:S(2)}) %all-to-all-start.1) | async-done | bytes 1048608 | tf_op jit(solution)/shard_map/all_to_all | solution.py:27
  126.3 33.8 %gather_fusion.2 = bf16[2048,128]{1,0:T(8,128)(2,1)} fusion(bf16[128,32,128]{2,1,0:T(8,128)(2,1)} %all-to-all-done.1, s32[2048]{0:T(1024)S(1)} %bitcast.38), kind=kCustom, calls=%fused_computation.2 | custom fusion | bytes 1064960 | tf_op jit(solution)/shard_map/gather | solution.py:97
  160.1 14.1 %gather_fusion.3 = bf16[6656,128]{1,0:T(8,128)(2,1)} fusion(bf16[2048,128]{1,0:T(8,128)(2,1)} %gather_fusion.2, s32[7168]{0:T(1024)S(1)} %pad_clamp_fusion), kind=kCustom, calls=%fused_computation.3 | custom fusion | bytes 3434496 | tf_op jit(solution)/shard_map/gather | solution.py:98
  174.2 4.4 reshape.123
  178.6 3.8 copy.45
  182.4 3.8 convolution_convert_fusion.1
  186.2 1.1 convolution_add_fusion
  187.3 0.3 copy-done.5
  187.6 1.1 convolution_add_fusion.1
  188.8 0.3 fusion.15
  189.1 1.2 fusion.19
  190.4 4.2 convolution_multiply_fusion.1
  194.6 1.1 convolution_convert_fusion
  195.7 4.0 convolution_multiply_fusion
  199.8 4.1 convolution_multiply_fusion.2
  203.9 0.7 copy-done.13
  204.7 0.1 copy.43
  204.8 0.1 reshape.166
  204.9 3.3 fusion.25
  208.2 0.8 copy-done.8
  209.0 2.4 slice_add_fusion
  211.5 3.5 copy.47
  214.9 1.9 reshape.168
  216.8 36.7 %scatter_custom_fusion = f32[2048,128]{1,0:T(8,128)S(1)} fusion(s32[6656]{0:T(1024)S(1)} %reshape.166, f32[6656,128]{1,0:T(8,128)} %reshape.168, f32[]{:T(128)} %constant.13.clone.1), kind=kCustom, calls=%fused_computation.45 | custom fusion | flops 851968 | bytes 1049088 | tf_op jit(solution)/shard_map/scatter-add | solution.py:105
  253.5 8.2 %scatter_custom_fusion.3 = f32[4096,128]{1,0:T(8,128)} fusion(s32[2048]{0:T(1024)} %get-tuple-element.21, f32[2048,128]{1,0:T(8,128)S(1)} %scatter_custom_fusion, f32[]{:T(128)} %constant.13.clone.1, f32[2048]{0:T(1024)S(1)} %convert_element_type.60), kind=kCustom, calls=%fused_computation.31 | custom fusion | flops 262144 | bytes 3154432
  261.7 6.6 %all-to-all-start.2 = ((f32[128,32,128]{2,1,0:T(8,128)}), f32[128,32,128]{2,1,0:T(8,128)S(1)}, u32[]{:S(2)}, u32[]{:S(2)}) async-start(f32[128,32,128]{2,1,0:T(8,128)} %bitcast.15), calls=%async_computation.2 | async-start | bytes 4194304 | tf_op jit(solution)/shard_map/all_to_all | solution.py:31
  268.3 0.5 broadcast.222
  268.8 0.8 reduce.10
  269.6 0.1 all_to_all.18
  269.7 1.3 broadcast_multiply_fusion
  271.0 26.3 %all-to-all-done.2 = f32[128,32,128]{2,1,0:T(8,128)S(1)} async-done(((f32[128,32,128]{2,1,0:T(8,128)}), f32[128,32,128]{2,1,0:T(8,128)S(1)}, u32[]{:S(2)}, u32[]{:S(2)}) %all-to-all-start.2) | async-done | bytes 2097184 | tf_op jit(solution)/shard_map/all_to_all | solution.py:31
  297.4 1.4 copy-done.11
  298.7 23.2 %scatter_custom_fusion.1 = f32[4096,128]{1,0:T(8,128)S(1)} fusion(s32[4096]{0:T(1024)S(1)} %bitcast.47, f32[4096,128]{1,0:T(8,128)} %bitcast.40, f32[]{:T(128)} %constant.13.clone.1), kind=kCustom, calls=%fused_computation.38 | custom fusion | flops 524288 | bytes 2097664 | tf_op jit(solution)/shard_map/scatter-add | solution.py:114
  321.9 1.3 copy-done.6
  323.3 0.6 multiply_reduce_fusion
  323.9 0.6 fusion.24
  324.5 3.4 abs_reduce_fusion
  327.9 1.5 divide_convert_fusion
  329.4 111.3 %all-reduce.6.cloned.1.call-done = (f32[512,3341]{1,0:T(8,128)}, f32[512,3341]{1,0:T(8,128)}, f32[512,3341]{1,0:T(8,128)}) async-done(((f32[512,3341]{1,0:T(8,128)}, f32[512,3341]{1,0:T(8,128)}, f32[512,3341]{1,0:T(8,128)}), (f32[512,3341]{1,0:T(8,128)}, f32[512,3341]{1,0:T(8,128)}, f32[512,3341]{1,0:T(8,128)})) %all-reduce.6.cloned.1.call-update) | async-done | bytes 20527120
  440.7 1.5 constant_dynamic-slice_fusion.2
  442.3 1.6 constant_dynamic-slice_fusion
  (61 shorter events, 0.3 us)
Async XLA Ops:
  7.2 180.1 %copy-start = (bf16[3341,512]{1,0:T(8,128)(2,1)S(1)}, bf16[3341,512]{1,0:T(8,128)(2,1)}, u32[]{:S(2)}) copy-start(bf16[3341,512]{1,0:T(8,128)(2,1)} %param.27) | copy-start | bytes 10263556
  7.2 4.7 %copy-start.24 = (s32[2]{0:T(128)S(1)}, s32[2]{0:T(128)}, u32[]{:S(2)}) copy-start(s32[2]{0:T(128)} %constant.51) | copy-start | bytes 28
  7.2 4.8 %copy-start.22 = (s32[2]{0:T(128)S(1)}, s32[2]{0:T(128)}, u32[]{:S(2)}) copy-start(s32[2]{0:T(128)} %constant.54) | copy-start | bytes 28
  7.2 4.8 %copy-start.23 = (s32[2]{0:T(128)S(1)}, s32[2]{0:T(128)}, u32[]{:S(2)}) copy-start(s32[2]{0:T(128)} %constant.11) | copy-start | bytes 28
  7.2 4.0 copy-start.14
  8.5 1.0 copy-start.9
  42.0 15.7 %copy-start.2 = (f32[4096]{0:T(1024)S(1)}, f32[4096]{0:T(1024)}, u32[]{:S(2)}) copy-start(f32[4096]{0:T(1024)} %param.22) | copy-start | bytes 49156
  98.3 10.6 %copy-start.20 = (bf16[512]{0:T(512)(128)(2,1)S(1)}, bf16[512]{0:T(512)(128)(2,1)}, u32[]{:S(2)}) copy-start(bf16[512]{0:T(512)(128)(2,1)} %param.29) | copy-start | bytes 3076
  102.3 24.0 %all-to-all-start.1 = ((bf16[128,32,128]{2,1,0:T(8,128)(2,1)}), bf16[128,32,128]{2,1,0:T(8,128)(2,1)}, u32[]{:S(2)}, u32[]{:S(2)}) async-start(bf16[128,32,128]{2,1,0:T(8,128)(2,1)} %fusion.2), calls=%async_computation.1 | async-start | bytes 2097152 | tf_op jit(solution)/shard_map/all_to_all | solution.py:27
  108.8 331.9 %all-reduce.6.cloned.1.call-start = ((), (), s32[]{:S(2)}) async-start(), calls=%async_computation.3 | async-start | bytes 42467328
  174.2 8.2 %copy-start.15 = (bf16[256,13]{0,1:T(8,128)(2,1)S(1)}, bf16[256,13]{0,1:T(8,128)(2,1)}, u32[]{:S(2)}) copy-start(bf16[256,13]{0,1:T(8,128)(2,1)} %param.15) | copy-start | bytes 19972
  182.4 3.8 copy-start.10
  182.4 3.8 copy-start.18
  186.2 1.5 copy-start.5
  186.2 1.4 copy-start.25
  187.6 2.7 copy-start.3
  187.6 1.4 copy-start.21
  190.3 5.4 %copy-start.7 = (f32[256,3341]{0,1:T(8,128)}, f32[256,3341]{0,1:T(8,128)S(1)}, u32[]{:S(2)}) copy-start(f32[256,3341]{0,1:T(8,128)S(1)} %fusion.19) | copy-start | bytes 10263556
  195.7 4.0 copy-start.12
  203.9 0.8 copy-start.13
  203.9 1.0 copy-start.17
  204.9 3.3 copy-start.4
  204.9 4.1 copy-start.8
  261.7 35.7 %all-to-all-start.2 = ((f32[128,32,128]{2,1,0:T(8,128)}), f32[128,32,128]{2,1,0:T(8,128)S(1)}, u32[]{:S(2)}, u32[]{:S(2)}) async-start(f32[128,32,128]{2,1,0:T(8,128)} %bitcast.15), calls=%async_computation.2 | async-start | bytes 4194304 | tf_op jit(solution)/shard_map/all_to_all | solution.py:31
  268.2 55.7 %copy-start.19 = (f32[4096]{0:T(1024)S(1)}, f32[4096]{0:T(1024)}, u32[]{:S(2)}) copy-start(f32[4096]{0:T(1024)} %param.23) | copy-start | bytes 49156
  297.4 1.4 copy-start.11
  321.9 1.4 copy-start.6
  324.5 119.4 %copy-start.1 = (bf16[3341,512]{1,0:T(8,128)(2,1)S(1)}, bf16[3341,512]{1,0:T(8,128)(2,1)}, u32[]{:S(2)}) copy-start(bf16[3341,512]{1,0:T(8,128)(2,1)} %param.27) | copy-start | bytes 10263556
  327.9 116.0 %copy-start.16 = (f32[4096]{0:T(1024)}, f32[4096]{0:T(1024)S(1)}, u32[]{:S(2)}) copy-start(f32[4096]{0:T(1024)S(1)} %add_multiply_fusion) | copy-start | bytes 49156
Sparse Core Ops, SparseCore 0:
  204.0 236.6 all-reduce.5
where the time goes:
time: 453 us; the launch traced here: 451 us
  waiting for transfers between devices  150 us (33%)
  local copies, waits for them, and re-layouts  143 us (32%)
  other arithmetic  87.2 us (19%)
  matrix products  24.3 us (5%)
  blocking collectives  18.7 us (4%)
  between operations  14.5 us (3%)
  starting transfers between devices  13.2 us (3%)
    unnamed x2, waiting for transfers between devices  111 us
    gather x2, local copies, waits for them, and re-layouts, on_device(): table_scale[row_index][:, :, None]  42 us
    scatter-add x1, other arithmetic, on_device(): jax.ops.segment_sum(emb_grad, slot_ids.reshape(-1), num_segments=need_rows)  36.7 us
    gather x1, local copies, waits for them, and re-layouts, on_device(): fetched = returned[owners, places]  33.8 us
    all_to_all x1, waiting for transfers between devices, send_grads(): lax.all_to_all(outgoing, ('hst', 'chip'), split_axis=0, concat_axis=0, ti...  26.3 us
    scatter-add x1, other arithmetic, on_device(): jax.ops.segment_sum(received.reshape(-1, emb_width), row_index.reshape(-1...  23.2 us
    all_to_all x1, blocking collectives, send_requests(): lax.all_to_all(requests, ('hst', 'chip'), split_axis=0, concat_axis=0, ti...  18.7 us
    unnamed x57, local copies, waits for them, and re-layouts  17.1 us
  transfers between devices with their start and end apart: 3, of which 3 were waited for; matrix products, arithmetic and copies ran while one was open for 21% of the time, Pallas kernels for 0%

commit v1 on v0

--- a/solution.py
+++ b/solution.py
@@ -1,8 +1,13 @@
+import functools
+
 import jax
+import jax.experimental.pallas as pl
+import jax.experimental.pallas.tpu as pltpu
 import jax.numpy as jnp
 from jax import lax
 from jax.sharding import PartitionSpec as P
 
+MESH = pl.DeviceIdType.MESH
 LEARN_RATE = 0.1
 QUANT_TOP = 4.0
 
@@ -17,6 +22,277 @@
     return lax.dot_general(
         left, right, (((0,), (0,)), ((), ())), preferred_element_type=jnp.float32
     )
+
+
+def coords():
+    host = lax.axis_index("hst")
+    chip = lax.axis_index("chip")
+    return host // 4, host % 4, chip // 2, chip % 2
+
+
+def hosts_from(y, z):
+    return [((y + d // 4) % 4) * 4 + (z + d % 4) % 4 for d in range(16)]
+
+
+def chips_from(x, core):
+    return [((x + d // 2) % 4) * 2 + (core + d % 2) % 2 for d in range(8)]
+
+
+def neg_host(d):
+    return ((4 - d // 4) % 4) * 4 + (4 - d % 4) % 4
+
+
+def neg_chip(d):
+    return ((4 - d // 2) % 4) * 2 + d % 2
+
+
+def greet_all(barrier):
+    y, z, x, core = coords()
+    chips = chips_from(x, core)
+
+    def one(d, _):
+        host = ((y + d // 4) % 4) * 4 + (z + d % 4) % 4
+        for e in range(8):
+            if e == 0:
+
+                @pl.when(d > 0)
+                def _():
+                    pl.semaphore_signal(barrier, inc=1, device_id=(host, chips[0]), device_id_type=MESH)
+
+            else:
+                pl.semaphore_signal(barrier, inc=1, device_id=(host, chips[e]), device_id_type=MESH)
+        return 0
+
+    lax.fori_loop(0, 16, one, 0)
+
+
+def hot(cond):
+    return jnp.where(cond, 1.0, 0.0).astype(jnp.bfloat16)
+
+
+def to_column(row):
+    return jnp.broadcast_to(row, (128, 128)).T
+
+
+def lane_tiles(col, count):
+    lane = lax.broadcasted_iota(jnp.int32, col.shape, 1)
+    return jnp.concatenate([hot(col == lane + 128 * i) for i in range(count)], axis=1)
+
+
+def embed_kernel(
+    owner_ref,
+    local_ref,
+    slots_ref,
+    rows_ref,
+    scale_ref,
+    base_ref,
+    pos_ref,
+    inc_out_ref,
+    req,
+    inc,
+    val,
+    ret,
+    table2,
+    qcol,
+    poscol,
+    fetched,
+    fetched2,
+    sidcol,
+    req_send,
+    req_recv,
+    val_send,
+    val_recv,
+):
+    y, z, x, core = coords()
+    chips = chips_from(x, core)
+    barrier = pltpu.get_barrier_semaphore()
+    greet_all(barrier)
+
+    owner = owner_ref[...]
+    rel = (
+        (((owner >> 5) - y) & 3) * 32
+        + (((owner >> 3) - z) & 3) * 8
+        + (((owner >> 1) - x) & 3) * 2
+        + ((owner - core) & 1)
+    )
+    sub = lax.broadcasted_iota(jnp.int32, (128, 256), 0)
+    upper = hot(
+        lax.broadcasted_iota(jnp.int32, (256, 256), 0) < lax.broadcasted_iota(jnp.int32, (256, 256), 1)
+    )
+    seen = jnp.zeros((128, 1), jnp.float32)
+    hi_sum = jnp.zeros((128, 32), jnp.float32)
+    lo_sum = jnp.zeros((128, 32), jnp.float32)
+    for i in range(8):
+        part = rel[:, 256 * i : 256 * i + 256]
+        hits = hot(part == sub)
+        before = jnp.dot(hits, upper, preferred_element_type=jnp.float32) + seen
+        wide = hits.astype(jnp.float32)
+        place = jnp.sum(wide * before, axis=0, keepdims=True).astype(jnp.int32)
+        seen = seen + jnp.sum(wide, axis=1, keepdims=True)
+        pos_ref[:, 256 * i : 256 * i + 256] = part * 32 + place
+        code = local_ref[:, 256 * i : 256 * i + 256] + 1
+        here = place == lax.broadcasted_iota(jnp.int32, (32, 256), 0)
+        hi = jnp.where(here, (code >> 6).astype(jnp.float32), 0.0).astype(jnp.bfloat16)
+        lo = jnp.where(here, (code & 63).astype(jnp.float32), 0.0).astype(jnp.bfloat16)
+        hi_sum = hi_sum + contract_last(hits, hi)
+        lo_sum = lo_sum + contract_last(hits, lo)
+    asked = (hi_sum * 64.0 + lo_sum).astype(jnp.int32) - 1
+    asked = jnp.concatenate([asked, jnp.full((128, 96), -1, jnp.int32)], axis=1)
+    for k in range(128):
+        req[k] = asked[k : k + 1, :]
+    inc[0] = req[0]
+
+    pl.semaphore_wait(barrier, 127)
+
+    def ask(d, _):
+        host = ((y + d // 4) % 4) * 4 + (z + d % 4) % 4
+        back = ((4 - d // 4) % 4) * 4 + (4 - d % 4) % 4
+        for e in range(8):
+
+            def go():
+                pltpu.make_async_remote_copy(
+                    src_ref=req.at[d * 8 + e],
+                    dst_ref=inc.at[back * 8 + neg_chip(e)],
+                    send_sem=req_send,
+                    recv_sem=req_recv,
+                    device_id=(host, chips[e]),
+                    device_id_type=MESH,
+                ).start()
+
+            if e == 0:
+                pl.when(d > 0)(go)
+            else:
+                go()
+        return 0
+
+    lax.fori_loop(0, 16, ask, 0)
+
+    for i in range(32):
+        rows = rows_ref[128 * i : 128 * i + 128, :].astype(jnp.float32)
+        col = to_column(scale_ref[i : i + 1, :])
+        table2[(i % 8) * 128 : (i % 8) * 128 + 128, (i // 8) * 128 : (i // 8) * 128 + 128] = (
+            rows * col
+        ).astype(jnp.bfloat16)
+    for i in range(16):
+        poscol[128 * i : 128 * i + 128, :] = to_column(pos_ref[:, 128 * i : 128 * i + 128])
+    ids = jnp.concatenate([slots_ref[...], jnp.zeros((6, 256), jnp.int32)], axis=0)
+    ids = jnp.concatenate([ids, jnp.zeros((96, 256), jnp.int32)], axis=0).T
+    for t in range(26):
+        sidcol[256 * t : 256 * t + 256, :] = jnp.broadcast_to(ids[:, t : t + 1], (256, 128))
+
+    pltpu.make_async_copy(req.at[pl.ds(0, 127)], req.at[pl.ds(0, 127)], req_send).wait()
+    pltpu.make_async_copy(inc.at[pl.ds(1, 127)], inc.at[pl.ds(1, 127)], req_recv).wait()
+    got = inc[...].reshape(128, 128)
+    inc_out_ref[...] = got
+    got_t = got.T
+    for k in range(128):
+        qcol[32 * k : 32 * k + 32, :] = jnp.broadcast_to(got_t[0:32, k : k + 1], (32, 128))
+
+    def serve(d, _):
+        host = ((y + d // 4) % 4) * 4 + (z + d % 4) % 4
+        back = ((4 - d // 4) % 4) * 4 + (4 - d % 4) % 4
+        at = pl.multiple_of(d * 256, 256)
+        query = qcol[pl.ds(at, 256), :]
+        found = jnp.dot(lane_tiles(query & 1023, 8), table2[...], preferred_element_type=jnp.float32)
+        quarter = query >> 10
+        out = jnp.zeros((256, 128), jnp.float32)
+        for i in range(4):
+            out = jnp.where(quarter == i, found[:, 128 * i : 128 * i + 128], out)
+        val[pl.ds(at, 256), :] = out.astype(jnp.bfloat16)
+        for e in range(8):
+
+            def go():
+                pltpu.make_async_remote_copy(
+                    src_ref=val.at[pl.ds(pl.multiple_of(at + 32 * e, 32), 32), :],
+                    dst_ref=ret.at[pl.ds(pl.multiple_of(back * 256 + 32 * neg_chip(e), 32), 32), :],
+                    send_sem=val_send,
+                    recv_sem=val_recv.at[back // 4],
+                    device_id=(host, chips[e]),
+                    device_id_type=MESH,
+                ).start()
+
+            if e == 0:
+                pl.when(d > 0)(go)
+            else:
+                go()
+        return 0
+
+    lax.fori_loop(0, 16, serve, 0)
+    ret[0:32, :] = val[0:32, :]
+    for chunk in (0, 3, 2, 1):
+        if chunk == 0:
+            landed = ret.at[pl.ds(32, 992), :]
+        else:
+            landed = ret.at[pl.ds(1024 * chunk, 1024), :]
+        pltpu.make_async_copy(landed, landed, val_recv.at[chunk]).wait()
+        pair = jnp.concatenate(
+            [ret[1024 * chunk : 1024 * chunk + 512, :], ret[1024 * chunk + 512 : 1024 * chunk + 1024, :]],
+            axis=1,
+        )
+
+        def pick(i, _):
+            at = pl.multiple_of(i * 256, 256)
+            where = poscol[pl.ds(at, 256), :]
+            found = jnp.dot(lane_tiles(where & 511, 4), pair, preferred_element_type=jnp.float32)
+            half = where >> 9
+            if chunk == 0:
+                out = jnp.zeros((256, 128), jnp.float32)
+            else:
+                out = fetched[pl.ds(at, 256), :]
+            out = jnp.where(half == 2 * chunk, found[:, :128], out)
+            fetched[pl.ds(at, 256), :] = jnp.where(half == 2 * chunk + 1, found[:, 128:], out)
+            return 0
+
+        lax.fori_loop(0, 8, pick, 0)
+    fetched2[:, 0:128] = fetched[0:1024, :].astype(jnp.bfloat16)
+    fetched2[:, 128:256] = fetched[1024:2048, :].astype(jnp.bfloat16)
+
+    def spread(t, _):
+        at = pl.multiple_of(t * 256, 256)
+        slot = sidcol[pl.ds(at, 256), :]
+        found = jnp.dot(lane_tiles(slot & 1023, 8), fetched2[...], preferred_element_type=jnp.float32)
+        base_ref[:, pl.ds(pl.multiple_of(t * 128, 128), 128)] = jnp.where(
+            slot < 1024, found[:, :128], found[:, 128:]
+        ).astype(jnp.bfloat16)
+        return 0
+
+    lax.fori_loop(0, 26, spread, 0)
+    sent = val.at[pl.ds(32, 4064), :]
+    pltpu.make_async_copy(sent, sent, val_send).wait()
+
+
+def embed(owner, local, slots_t, rows, scale):
+    vmem = pl.BlockSpec(memory_space=pltpu.VMEM)
+    return pl.pallas_call(
+        embed_kernel,
+        name="embed",
+        out_shape=(
+            jax.ShapeDtypeStruct((256, 3328), jnp.bfloat16),
+            jax.ShapeDtypeStruct((1, 2048), jnp.int32),
+            jax.ShapeDtypeStruct((128, 128), jnp.int32),
+        ),
+        in_specs=[vmem] * 5,
+        out_specs=(vmem,) * 3,
+        scratch_shapes=[
+            pltpu.VMEM((128, 1, 128), jnp.int32),
+            pltpu.VMEM((128, 1, 128), jnp.int32),
+            pltpu.VMEM((4096, 128), jnp.bfloat16),
+            pltpu.VMEM((4096, 128), jnp.bfloat16),
+            pltpu.VMEM((1024, 512), jnp.bfloat16),
+            pltpu.VMEM((4096, 128), jnp.int32),
+            pltpu.VMEM((2048, 128), jnp.int32),
+            pltpu.VMEM((2048, 128), jnp.float32),
+            pltpu.VMEM((1024, 256), jnp.bfloat16),
+            pltpu.VMEM((6656, 128), jnp.int32),
+            pltpu.SemaphoreType.DMA,
+            pltpu.SemaphoreType.DMA,
+            pltpu.SemaphoreType.DMA,
+            pltpu.SemaphoreType.DMA((4,)),
+        ],
+        compiler_params=pltpu.CompilerParams(
+            collective_id=0, has_side_effects=True, vmem_limit_bytes=48 * 2**20
+        ),
+    )(owner, local, slots_t, rows, scale)
 
 
 def send_requests(requests):
@@ -90,12 +366,13 @@
     requests = jnp.full((devices, capacity), -1, jnp.int32).at[owners, places].set(needed_local)
     incoming = send_requests(requests)
     row_index = jnp.where(incoming >= 0, incoming, 0)
-    served = (
-        table_rows[row_index].astype(jnp.float32) * table_scale[row_index][:, :, None]
-    ).astype(jnp.bfloat16)
-    returned = send_values(served)
-    fetched = returned[owners, places]
-    embedded = fetched[slot_ids].reshape(batch_rows, -1)
+    embedded, _, _ = embed(
+        owners.reshape(1, -1),
+        needed_local.reshape(1, -1),
+        slot_ids.T,
+        table_rows,
+        table_scale.reshape(32, 128),
+    )
     base_in = jnp.concatenate([embedded, dense_feats], axis=1)
     low_rank, crossed, grad_hidden, grad_mix, grad_low, grad_input = dense_step(
         base_in, labels, cross_down, cross_up, cross_bias, hidden_weight, hidden_bias, out_weight

time: 453 us -> 340 us (0.75)
  local copies, waits for them, and re-layouts: 143 us -> 28.3 us
  Pallas kernels: 0 us -> 48.3 us
  waiting for transfers between devices: 150 us -> 124 us
  blocking collectives: 18.7 us -> 0 us
  other arithmetic: 87.2 us -> 82 us
    gather x5 -> x0, local copies, waits for them, and re-layouts: 106 us -> none  [the longest x2 42 us: on_device(): table_scale[row_index][:, :, None]]
    pallas_call x0 -> x1, Pallas kernels: none -> 48.3 us  [embed(): pl.pallas_call(embed_kernel, name='embed', out_shape=(jax.ShapeDtypeStruc...]
    all_to_all x1 -> x0, blocking collectives: 18.7 us -> none  [send_requests(): lax.all_to_all(requests, ('hst', 'chip'), split_axis=0, concat_axis=0, ti...]
    unnamed x2, waiting for transfers between devices: 111 us -> 97 us
    all_to_all x1, waiting for transfers between devices: 12 us -> 0.01 us  [send_requests(): lax.all_to_all(requests, ('hst', 'chip'), split_axis=0, concat_axis=0, ti...]
    reshape x2 -> x0, local copies, waits for them, and re-layouts: 8.16 us -> none  [on_device(): embedded = fetched[slot_ids].reshape(batch_rows, -1)]
    unnamed x57 -> x58, local copies, waits for them, and re-layouts: 17.1 us -> 21.8 us
  transfers between devices with their start and end apart: 3 -> 3, of which waited for: 3 -> 2; matrix products, arithmetic and copies ran while one was open for 21% -> 29% of each run, Pallas kernels for 0% -> 0%
where the time goes in v1:
time: 340 us; the launch traced here: 338 us
  waiting for transfers between devices  124 us (36%)
  other arithmetic  82 us (24%)
  Pallas kernels  48.3 us (14%)
  local copies, waits for them, and re-layouts  28.3 us (8%)
  matrix products  24 us (7%)
  starting transfers between devices  16.8 us (5%)
  between operations  14.5 us (4%)
    unnamed x2, waiting for transfers between devices  97 us
    pallas_call x1, Pallas kernels, embed(): pl.pallas_call(embed_kernel, name='embed', out_shape=(jax.ShapeDtypeStruc...  48.3 us
    scatter-add x1, other arithmetic, on_device(): jax.ops.segment_sum(emb_grad, slot_ids.reshape(-1), num_segments=need_rows)  36.5 us
    all_to_all x1, waiting for transfers between devices, send_grads(): lax.all_to_all(outgoing, ('hst', 'chip'), split_axis=0, concat_axis=0, ti...  27 us
    scatter-add x1, other arithmetic, on_device(): jax.ops.segment_sum(received.reshape(-1, emb_width), row_index.reshape(-1...  24.9 us
    unnamed x58, local copies, waits for them, and re-layouts  21.8 us
    dot_general x3, matrix products, contract_first(): lax.dot_general(left, right, (((0,), (0,)), ((), ())), preferred_element_...  12.4 us
    all_to_all x1, starting transfers between devices, send_grads(): lax.all_to_all(outgoing, ('hst', 'chip'), split_axis=0, concat_axis=0, ti...  9.73 us
  transfers between devices with their start and end apart: 3, of which 2 were waited for; matrix products, arithmetic and copies ran while one was open for 29% of the time, Pallas kernels for 0%

profile of v1, /device:TPU:6, one launch (start us, length us, event | category | flops | bytes accessed | tf_op | source)
XLA Modules:
  0.0 337.9 jit_solution(9885557434489848013)
XLA Ops:
  7.2 0.0 copy-start
  7.2 0.0 all-reduce.6.cloned.1.call-start
  7.2 0.8 convert_element_type.48
  8.1 0.8 reshape.138
  8.9 0.8 copy.46
  9.7 1.2 copy-done.2
  11.0 0.7 copy-done.3
  11.7 0.8 copy-done.5
  12.4 0.7 copy-done.7
  13.1 0.7 copy-done.9
  13.8 48.3 %embed.1 = (bf16[256,3328]{1,0:T(8,128)(2,1)S(1)}, s32[1,2048]{1,0:T(1,128)}, s32[128,128]{1,0:T(8,128)}) custom-call(s32[1,2048]{1,0:T(1,128)S(1)} %bitcast.36, s32[1,2048]{1,0:T(1,128)S(1)} %bitcast.41, s32[26,256]{1,0:T(8,128)S(1)} %bitcast.39, bf16[4096,128]{1,0:T(8,128)(2,1)S(1)} %copy-done.2, f32[32,128]{1,0:T(8,128)S(1)} %bitcast.40), custom_call_target="tpu_custom_call" | custom-call | tf_op jit(solution)/shard_map/embed/pallas_call | solution.py:266
  62.1 0.0 copy-start.15
  62.1 0.0 copy-start.17
  62.1 3.2 convolution_convert_fusion.1
  65.4 0.0 copy-start.25
  65.4 1.2 convolution_add_fusion
  66.7 1.2 convolution_add_fusion.1
  67.9 0.3 fusion.14
  68.1 1.3 fusion.18
  69.4 4.2 %convolution_multiply_fusion.1 = f32[512,3341]{1,0:T(8,128)} fusion(f32[256,512]{1,0:T(8,128)S(1)} %convolution_add_fusion.1, f32[512]{0:T(512)S(1)} %convert_element_type.48, f32[256]{0:T(256)S(1)} %divide_subtract_fusion.1, f32[256,3341]{1,0:T(8,128)S(1)} %convolution_add_fusion, bf16[256,13]{1,0:T(8,128)(2,1)S(1)} %copy.46, ...), kind=kOutput, calls=%fused_computation.5 | convolution fusion | flops 884831488 | bytes 12501504 | tf_op jit(solution)/shard_map/dot_general | solution.py:22
  73.7 1.2 convolution_convert_fusion
  74.9 4.1 %convolution_multiply_fusion = f32[512,3341]{1,0:T(8,128)} fusion(bf16[256,512]{1,0:T(8,128)(2,1)S(1)} %convolution_convert_fusion.1, f32[256,3341]{1,0:T(8,128)S(1)} %fusion.18, bf16[256,13]{1,0:T(8,128)(2,1)S(1)} %copy.46, bf16[256,3328]{1,0:T(8,128)(2,1)S(1)} %get-tuple-element.8), kind=kOutput, calls=%fused_computation.4 | convolution fusion | flops 882665472 | bytes 12236288 | tf_op jit(solution)/shard_map/dot_general | solution.py:22
  78.9 4.1 %convolution_multiply_fusion.2 = f32[512,3341]{1,0:T(8,128)} fusion(bf16[256,512]{1,0:T(8,128)(2,1)S(1)} %convolution_convert_fusion, bf16[256,13]{1,0:T(8,128)(2,1)S(1)} %copy.46, bf16[256,3328]{1,0:T(8,128)(2,1)S(1)} %get-tuple-element.8), kind=kOutput, calls=%fused_computation.6 | convolution fusion | flops 880954880 | bytes 8815104 | tf_op jit(solution)/shard_map/dot_general | solution.py:22
  83.0 0.0 all-reduce.6.cloned.1.call-update
  83.1 0.0 copy-start.24
  83.1 0.0 copy-start.22
  83.1 0.0 copy-start.23
  83.1 0.6 copy-done.4
  83.7 0.1 copy.42
  83.8 0.3 fusion.5
  84.2 0.1 broadcast_add_fusion
  84.3 0.3 copy.43
  84.6 0.6 fusion.2
  85.3 0.1 and_reduce_fusion
  85.5 0.1 multiply_reduce_fusion.1
  85.6 8.2 %scatter_custom_fusion.2 = s32[4096]{0:T(1024)S(1)} fusion(s32[2048]{0:T(1024)S(1)} %get-tuple-element.21, s32[2048]{0:T(1024)} %param.19, s32[]{:T(128)} %constant.12.clone.1), kind=kCustom, calls=%fused_computation.54 | custom fusion | bytes 16896
  93.8 0.7 copy.44
  94.6 7.0 %all-to-all-start = ((s32[128,1,32]{2,1,0:T(1,128)}), s32[128,1,32]{2,1,0:T(1,128)S(1)}, u32[]{:S(2)}, u32[]{:S(2)}) async-start(s32[128,1,32]{2,1,0:T(1,128)} %copy.44), calls=%async_computation | async-start | bytes 131072 | tf_op jit(solution)/shard_map/all_to_all | solution.py:299
  101.6 3.3 fusion.24
  104.9 1.1 copy-done.13
  106.0 2.2 slice_add_fusion
  108.2 0.1 copy.45
  108.3 0.1 reshape.111
  108.4 4.6 %reshape.113 = f32[6656,128]{1,0:T(8,128)} reshape(f32[256,3328]{1,0:T(8,128)} %slice_add_fusion) | data formatting | bytes 6815744 | tf_op jit(solution)/shard_map/reshape | solution.py:381
  113.1 36.5 %scatter_custom_fusion = f32[2048,128]{1,0:T(8,128)S(1)} fusion(s32[6656]{0:T(1024)S(1)} %reshape.111, f32[6656,128]{1,0:T(8,128)} %reshape.113, f32[]{:T(128)} %constant.11.clone.1), kind=kCustom, calls=%fused_computation.39 | custom fusion | flops 851968 | bytes 1049088 | tf_op jit(solution)/shard_map/scatter-add | solution.py:382
  149.5 8.1 %scatter_custom_fusion.3 = f32[4096,128]{1,0:T(8,128)} fusion(s32[2048]{0:T(1024)S(1)} %get-tuple-element.20, f32[2048,128]{1,0:T(8,128)S(1)} %scatter_custom_fusion, f32[]{:T(128)} %constant.11.clone.1, f32[2048]{0:T(1024)S(1)} %convert_element_type.52), kind=kCustom, calls=%fused_computation.25 | custom fusion | flops 262144 | bytes 3153924
  157.6 9.7 %all-to-all-start.1 = ((f32[128,32,128]{2,1,0:T(8,128)}), f32[128,32,128]{2,1,0:T(8,128)S(1)}, u32[]{:S(2)}, u32[]{:S(2)}) async-start(f32[128,32,128]{2,1,0:T(8,128)} %bitcast.16), calls=%async_computation.1 | async-start | bytes 4194304 | tf_op jit(solution)/shard_map/all_to_all | solution.py:307
  167.3 0.0 copy-start.20
  167.3 0.0 copy-start.8
  167.4 1.3 broadcast_multiply_fusion
  168.7 0.5 broadcast.148
  169.2 0.8 reduce.10
  170.0 0.1 all_to_all.13
  170.1 27.0 %all-to-all-done.1 = f32[128,32,128]{2,1,0:T(8,128)S(1)} async-done(((f32[128,32,128]{2,1,0:T(8,128)}), f32[128,32,128]{2,1,0:T(8,128)S(1)}, u32[]{:S(2)}, u32[]{:S(2)}) %all-to-all-start.1) | async-done | bytes 2097184 | tf_op jit(solution)/shard_map/all_to_all | solution.py:307
  197.1 1.4 copy-done.16
  198.5 24.9 %scatter_custom_fusion.1 = f32[4096,128]{1,0:T(8,128)S(1)} fusion(s32[4096]{0:T(1024)S(1)} %bitcast.46, f32[4096,128]{1,0:T(8,128)} %bitcast.42, f32[]{:T(128)} %constant.11.clone.1), kind=kCustom, calls=%fused_computation.32 | custom fusion | flops 524288 | bytes 2097664 | tf_op jit(solution)/shard_map/scatter-add | solution.py:391
  223.4 1.3 copy-done.14
  224.8 0.6 multiply_reduce_fusion
  225.4 0.6 fusion.23
  226.0 3.3 abs_reduce_fusion
  229.4 1.5 divide_convert_fusion
  230.9 97.0 %all-reduce.6.cloned.1.call-done = (f32[512,3341]{1,0:T(8,128)}, f32[512,3341]{1,0:T(8,128)}, f32[512,3341]{1,0:T(8,128)}) async-done(((f32[512,3341]{1,0:T(8,128)}, f32[512,3341]{1,0:T(8,128)}, f32[512,3341]{1,0:T(8,128)}), (f32[512,3341]{1,0:T(8,128)}, f32[512,3341]{1,0:T(8,128)}, f32[512,3341]{1,0:T(8,128)})) %all-reduce.6.cloned.1.call-update) | async-done | bytes 20527120
  327.9 1.5 constant_dynamic-slice_fusion.2
  329.4 1.6 constant_dynamic-slice_fusion
  (46 shorter events, 0.2 us)
Async XLA Ops:
  7.2 59.4 %copy-start = (bf16[3341,512]{1,0:T(8,128)(2,1)S(1)}, bf16[3341,512]{1,0:T(8,128)(2,1)}, u32[]{:S(2)}) copy-start(bf16[3341,512]{1,0:T(8,128)(2,1)} %param.27) | copy-start | bytes 10263556
  7.2 320.7 %all-reduce.6.cloned.1.call-start = ((), (), s32[]{:S(2)}) async-start(), calls=%async_computation.2 | async-start | bytes 42467328
  9.7 1.2 copy-start.2
  11.0 0.7 copy-start.3
  11.7 0.8 copy-start.5
  12.4 0.7 copy-start.7
  13.1 0.7 copy-start.9
  62.1 3.3 copy-start.15
  62.1 3.3 copy-start.17
  65.4 1.2 copy-start.25
  66.6 2.8 copy-start.12
  66.6 1.5 copy-start.21
  69.4 5.4 %copy-start.10 = (f32[256,3341]{1,0:T(8,128)}, f32[256,3341]{1,0:T(8,128)S(1)}, u32[]{:S(2)}) copy-start(f32[256,3341]{1,0:T(8,128)S(1)} %fusion.18) | copy-start | bytes 10263556
  83.0 0.7 copy-start.4
  83.1 2.3 copy-start.24
  83.1 2.4 copy-start.22
  83.1 2.4 copy-start.23
  94.6 63.0 %all-to-all-start = ((s32[128,1,32]{2,1,0:T(1,128)}), s32[128,1,32]{2,1,0:T(1,128)S(1)}, u32[]{:S(2)}, u32[]{:S(2)}) async-start(s32[128,1,32]{2,1,0:T(1,128)} %copy.44), calls=%async_computation | async-start | bytes 131072 | tf_op jit(solution)/shard_map/all_to_all | solution.py:299
  101.6 3.3 copy-start.11
  101.6 4.4 %copy-start.13 = (f32[256,3341]{1,0:T(8,128)S(1)}, f32[256,3341]{1,0:T(8,128)}, u32[]{:S(2)}) copy-start(f32[256,3341]{1,0:T(8,128)} %copy-done.12) | copy-start | bytes 10263556
  106.0 2.2 copy-start.6
  108.4 4.6 %copy-start.19 = (s32[2048]{0:T(1024)S(1)}, s32[2048]{0:T(1024)}, u32[]{:S(2)}) copy-start(s32[2048]{0:T(1024)} %param.20) | copy-start | bytes 24580
  157.6 39.5 %all-to-all-start.1 = ((f32[128,32,128]{2,1,0:T(8,128)}), f32[128,32,128]{2,1,0:T(8,128)S(1)}, u32[]{:S(2)}, u32[]{:S(2)}) async-start(f32[128,32,128]{2,1,0:T(8,128)} %bitcast.16), calls=%async_computation.1 | async-start | bytes 4194304 | tf_op jit(solution)/shard_map/all_to_all | solution.py:307
  167.3 58.0 %copy-start.20 = (f32[4096]{0:T(1024)S(1)}, f32[4096]{0:T(1024)}, u32[]{:S(2)}) copy-start(f32[4096]{0:T(1024)} %param.23) | copy-start | bytes 49156
  167.3 58.7 %copy-start.8 = (f32[4096]{0:T(1024)S(1)}, f32[4096]{0:T(1024)}, u32[]{:S(2)}) copy-start(f32[4096]{0:T(1024)} %param.22) | copy-start | bytes 49156
  197.1 1.4 copy-start.16
  223.4 1.4 copy-start.14
  226.0 105.1 %copy-start.1 = (bf16[3341,512]{1,0:T(8,128)(2,1)S(1)}, bf16[3341,512]{1,0:T(8,128)(2,1)}, u32[]{:S(2)}) copy-start(bf16[3341,512]{1,0:T(8,128)(2,1)} %param.27) | copy-start | bytes 10263556
  229.4 101.7 %copy-start.18 = (f32[4096]{0:T(1024)}, f32[4096]{0:T(1024)S(1)}, u32[]{:S(2)}) copy-start(f32[4096]{0:T(1024)S(1)} %add_multiply_fusion) | copy-start | bytes 49156
Sparse Core Ops, SparseCore 0:
  83.2 244.6 all-reduce.5

commit v2 on v1

--- a/solution.py
+++ b/solution.py
@@ -85,6 +85,7 @@
     slots_ref,
     rows_ref,
     scale_ref,
+    feats_ref,
     base_ref,
     pos_ref,
     inc_out_ref,
@@ -257,21 +258,22 @@
         return 0
 
     lax.fori_loop(0, 26, spread, 0)
+    base_ref[:, 3328:3584] = feats_ref[...]
     sent = val.at[pl.ds(32, 4064), :]
     pltpu.make_async_copy(sent, sent, val_send).wait()
 
 
-def embed(owner, local, slots_t, rows, scale):
+def embed(owner, local, slots_t, rows, scale, feats):
     vmem = pl.BlockSpec(memory_space=pltpu.VMEM)
     return pl.pallas_call(
         embed_kernel,
         name="embed",
         out_shape=(
-            jax.ShapeDtypeStruct((256, 3328), jnp.bfloat16),
+            jax.ShapeDtypeStruct((256, 3584), jnp.bfloat16),
             jax.ShapeDtypeStruct((1, 2048), jnp.int32),
             jax.ShapeDtypeStruct((128, 128), jnp.int32),
         ),
-        in_specs=[vmem] * 5,
+        in_specs=[vmem] * 6,
         out_specs=(vmem,) * 3,
         scratch_shapes=[
             pltpu.VMEM((128, 1, 128), jnp.int32),
@@ -292,46 +294,436 @@
         compiler_params=pltpu.CompilerParams(
             collective_id=0, has_side_effects=True, vmem_limit_bytes=48 * 2**20
         ),
-    )(owner, local, slots_t, rows, scale)
-
-
-def send_requests(requests):
-    return lax.all_to_all(requests, ("hst", "chip"), split_axis=0, concat_axis=0, tiled=True)
-
-
-def send_values(served):
-    return lax.all_to_all(served, ("hst", "chip"), split_axis=0, concat_axis=0, tiled=True)
-
-
-def send_grads(outgoing):
-    return lax.all_to_all(outgoing, ("hst", "chip"), split_axis=0, concat_axis=0, tiled=True)
-
-
-def dense_step(
-    base_in, labels, cross_down, cross_up, cross_bias, hidden_weight, hidden_bias, out_weight
+    )(owner, local, slots_t, rows, scale, feats)
+
+
+def dense_kernel(
+    base_ref,
+    labels_ref,
+    down_hbm,
+    up_hbm,
+    hid_hbm,
+    tails_ref,
+    bias_ref,
+    hid_bias_ref,
+    out_w_ref,
+    grad_ref,
+    crossed_ref,
+    mix_ref,
+    low_ref,
+    grad_hid_ref,
+    grad_low_ref,
+    down,
+    up,
+    hid,
+    factor,
+    sems,
 ):
-    low_rank = jnp.dot(base_in, cross_down, preferred_element_type=jnp.float32).astype(jnp.bfloat16)
-    mixing = jnp.dot(low_rank, cross_up, preferred_element_type=jnp.float32)
-    base_wide = base_in.astype(jnp.float32)
-    crossed = (base_wide * (mixing + cross_bias[None, :]) + base_wide).astype(jnp.bfloat16)
+    copies = []
+    for i, (src, dst) in enumerate(((down_hbm, down), (up_hbm, up), (hid_hbm, hid))):
+        copy = pltpu.make_async_copy(
+            src.at[pl.ds(0, 3328), :], dst.at[pl.ds(0, 3328), :], sems.at[i]
+        )
+        copy.start()
+        copies.append(copy)
+        dst[3328:3584, :] = tails_ref[:, 512 * i : 512 * i + 512]
+    copies[0].wait()
+    low_ref[...] = jnp.dot(base_ref[...], down[...], preferred_element_type=jnp.float32).astype(
+        jnp.bfloat16
+    )
+    copies[1].wait()
+
+    def cross(j, _):
+        at = pl.multiple_of(j * 256, 256)
+        cols = pl.ds(at, 256)
+        mixing = contract_last(low_ref[...], up[cols, :]) + bias_ref[:, cols]
+        base = base_ref[:, cols].astype(jnp.float32)
+        crossed_ref[:, cols] = (base * mixing + base).astype(jnp.bfloat16)
+        factor[:, cols] = mixing + 1.0
+        return 0
+
+    lax.fori_loop(0, 14, cross, 0)
+    copies[2].wait()
     preact = (
-        jnp.dot(crossed, hidden_weight, preferred_element_type=jnp.float32) + hidden_bias[None, :]
-    )
-    sig_pre = jax.nn.sigmoid(preact)
-    hidden = (preact * sig_pre).astype(jnp.bfloat16)
-    logits = jnp.dot(hidden, out_weight, preferred_element_type=jnp.float32)
-    grad_logit = jax.nn.sigmoid(logits) - labels.astype(jnp.float32)
-    slope = sig_pre * (1.0 + preact * (1.0 - sig_pre))
-    grad_hidden = (grad_logit[:, None] * out_weight.astype(jnp.float32)[None, :] * slope).astype(
+        jnp.dot(crossed_ref[...], hid[...], preferred_element_type=jnp.float32) + hid_bias_ref[...]
+    )
+    sig = jax.nn.sigmoid(preact)
+    hidden = (preact * sig).astype(jnp.bfloat16).astype(jnp.float32)
+    out_w = out_w_ref[...]
+    logits = jnp.sum(hidden * out_w, axis=1, keepdims=True)
+    labels = jnp.concatenate(
+        [to_column(labels_ref[:, 0:128]), to_column(labels_ref[:, 128:256])], axis=0
+    )[:, 0:1]
+    grad_logit = jax.nn.sigmoid(logits) - labels
+    grad_hid_ref[...] = (grad_logit * out_w * (sig * (1.0 + preact * (1.0 - sig)))).astype(
         jnp.bfloat16
     )
-    grad_cross = contract_last(grad_hidden, hidden_weight)
-    grad_mix = (grad_cross * base_wide).astype(jnp.bfloat16)
-    grad_low = contract_last(grad_mix, cross_up).astype(jnp.bfloat16)
-    grad_input = grad_cross * (mixing + cross_bias[None, :] + 1.0) + contract_last(
-        grad_low, cross_down
-    )
-    return (low_rank, crossed, grad_hidden, grad_mix, grad_low, grad_input)
+
+    def back(j, _):
+        at = pl.multiple_of(j * 256, 256)
+        cols = pl.ds(at, 256)
+        grad_cross = contract_last(grad_hid_ref[...], hid[cols, :])
+        mix_ref[:, cols] = (grad_cross * base_ref[:, cols].astype(jnp.float32)).astype(jnp.bfloat16)
+        factor[:, cols] = grad_cross * factor[:, cols]
+        return 0
+
+    lax.fori_loop(0, 14, back, 0)
+    grad_low_ref[...] = jnp.dot(mix_ref[...], up[...], preferred_element_type=jnp.float32).astype(
+        jnp.bfloat16
+    )
+
+    def last(j, _):
+        at = pl.multiple_of(j * 256, 256)
+        cols = pl.ds(at, 256)
+        grad = factor[:, cols] + contract_last(grad_low_ref[...], down[cols, :])
+        grad_ref[:, cols] = grad.astype(jnp.bfloat16)
+        return 0
+
+    lax.fori_loop(0, 13, last, 0)
+
+
+def dense(base, labels, down, up_t, hid, tails, bias, hid_bias, out_w):
+    vmem = pl.BlockSpec(memory_space=pltpu.VMEM)
+    anywhere = pl.BlockSpec(memory_space=pl.ANY)
+    wide = jax.ShapeDtypeStruct((256, 3584), jnp.bfloat16)
+    thin = jax.ShapeDtypeStruct((256, 512), jnp.bfloat16)
+    return pl.pallas_call(
+        dense_kernel,
+        name="dense",
+        out_shape=(jax.ShapeDtypeStruct((256, 3328), jnp.bfloat16), wide, wide, thin, thin, thin),
+        in_specs=[vmem, vmem, anywhere, anywhere, anywhere, vmem, vmem, vmem, vmem],
+        out_specs=(vmem,) * 6,
+        scratch_shapes=[
+            pltpu.VMEM((3584, 512), jnp.bfloat16),
+            pltpu.VMEM((3584, 512), jnp.bfloat16),
+            pltpu.VMEM((3584, 512), jnp.bfloat16),
+            pltpu.VMEM((256, 3584), jnp.float32),
+            pltpu.SemaphoreType.DMA((3,)),
+        ],
+        compiler_params=pltpu.CompilerParams(vmem_limit_bytes=48 * 2**20),
+        cost_estimate=pl.CostEstimate(
+            flops=6 * 2 * 256 * 3584 * 512, bytes_accessed=18 * 2**20, transcendentals=0
+        ),
+    )(base, labels, down, up_t, hid, tails, bias, hid_bias, out_w)
+
+
+AXES = (("y", "z", "x"), ("z", "x", "y"), ("x", "y", "z"))
+LEFT_OF = (0, 1, 2)
+
+
+def row_order(array, me):
+    row = lax.broadcasted_iota(jnp.int32, (512, 512), 0)
+    at = {"core": (me["core"] + (row >> 8)) & 1}
+    for stage, axis in enumerate(AXES[array]):
+        at[axis] = (me[axis] + (row >> (6 - 2 * stage))) & 3
+    source = (at["y"] * 32 + at["z"] * 8 + at["x"] * 2 + at["core"]) * 4 + (row & 3)
+    return hot(source == lax.broadcasted_iota(jnp.int32, (512, 512), 1))
+
+
+def shifted(me, axis, step):
+    to = dict(me)
+    to[axis] = (me[axis] + step) % 4
+    return (to["y"] * 4 + to["z"], to["x"] * 2 + to["core"])
+
+
+def update_kernel(
+    grad_ref,
+    base_ref,
+    crossed_ref,
+    mix_ref,
+    low_ref,
+    grad_hid_ref,
+    grad_low_ref,
+    pos_ref,
+    inc_ref,
+    slots_ref,
+    evict_ref,
+    rows_ref,
+    scale_ref,
+    acc_ref,
+    new_rows_ref,
+    new_scale_ref,
+    new_acc_ref,
+    cache_ref,
+    out_down_ref,
+    out_hid_ref,
+    out_up_ref,
+    split,
+    placed,
+    out,
+    rcv,
+    spread,
+    mine,
+    theirs,
+    lefts,
+    rights,
+    part,
+    first,
+    second_src,
+    second,
+    third_src,
+    third,
+    pair_send,
+    pair_recv,
+    grad_send,
+    grad_recv,
+    sum_send,
+    sum_recv,
+):
+    y, z, x, core = coords()
+    me = {"y": y, "z": z, "x": x, "core": core}
+    chips = chips_from(x, core)
+    barrier = pltpu.get_barrier_semaphore()
+    greet_all(barrier)
+
+    ids = jnp.concatenate([slots_ref[...], jnp.zeros((102, 256), jnp.int32)], axis=0).T
+    for t in range(26):
+        half = jnp.broadcast_to(ids[:, t : t + 1] >> 10, (256, 128))
+        grad = grad_ref[:, 128 * t : 128 * t + 128].astype(jnp.float32)
+        split[256 * t : 256 * t + 256, 0:128] = jnp.where(half == 0, grad, 0.0).astype(jnp.bfloat16)
+        split[256 * t : 256 * t + 256, 128:256] = jnp.where(half == 1, grad, 0.0).astype(
+            jnp.bfloat16
+        )
+    factors = (grad_low_ref, grad_hid_ref, low_ref)
+    wides = (base_ref, crossed_ref, mix_ref)
+    for a in range(3):
+        order = row_order(a, me)
+        mine[a] = contract_last(order[0:256], factors[a][...]).astype(jnp.bfloat16)
+        theirs[a] = contract_last(order[256:512], factors[a][...]).astype(jnp.bfloat16)
+
+    pl.semaphore_wait(barrier, 127)
+    partner = (y * 4 + z, x * 2 + 1 - core)
+    pair = []
+    for a in range(3):
+        for i, (src, dst) in enumerate(((theirs.at[a], lefts.at[a]), (wides[a], rights.at[a]))):
+            copy = pltpu.make_async_remote_copy(
+                src_ref=src,
+                dst_ref=dst,
+                send_sem=pair_send.at[a, i],
+                recv_sem=pair_recv.at[a, i],
+                device_id=partner,
+                device_id_type=MESH,
+            )
+            copy.start()
+            pair.append(copy)
+
+    def slots(m, _):
+        at = pl.multiple_of(m * 256, 256)
+        slot = lax.broadcasted_iota(jnp.int32, (256, 256), 0) + at
+        picks = jnp.concatenate(
+            [hot(slot == (slots_ref[t : t + 1, :] & 1023)) for t in range(26)], axis=1
+        )
+        sums = jnp.dot(picks, split[...], preferred_element_type=jnp.float32)
+        for side in range(2):
+            for block in range(2):
+                i = side * 8 + m * 2 + block
+                here = pl.ds(pl.multiple_of(i * 128, 128), 128)
+                total = sums[128 * block : 128 * block + 128, 128 * side : 128 * side + 128]
+                gone = to_column(evict_ref[pl.ds(i, 1), :].astype(jnp.float32))
+                cache_ref[here, :] = total * (1.0 - gone)
+                sent = total * gone
+                upper = to_column(pos_ref[pl.ds(i, 1), :]) >> 11
+                placed[here, 0:128] = jnp.where(upper == 0, sent, 0.0).astype(jnp.bfloat16)
+                placed[here, 128:256] = jnp.where(upper == 1, sent, 0.0).astype(jnp.bfloat16)
+        return 0
+
+    lax.fori_loop(0, 4, slots, 0)
+
+    def send(j, _):
+        at = pl.multiple_of(j * 256, 256)
+        place = lax.broadcasted_iota(jnp.int32, (256, 128), 0) + at
+        picks = jnp.concatenate(
+            [hot(place == (pos_ref[i : i + 1, :] & 2047)) for i in range(16)], axis=1
+        )
+        sums = jnp.dot(picks, placed[...], preferred_element_type=jnp.float32)
+        for side in range(2):
+            d = j + 8 * side
+            start = pl.multiple_of(d * 256, 256)
+            out[pl.ds(start, 256), :] = sums[:, 128 * side : 128 * side + 128].astype(jnp.bfloat16)
+            host = ((y + d // 4) % 4) * 4 + (z + d % 4) % 4
+            back = ((4 - d // 4) % 4) * 4 + (4 - d % 4) % 4
+            for e in range(8):
+
+                def go():
+                    pltpu.make_async_remote_copy(
+                        src_ref=out.at[pl.ds(pl.multiple_of(start + 32 * e, 32), 32), :],
+                        dst_ref=rcv.at[
+                            pl.ds(pl.multiple_of(back * 256 + 32 * neg_chip(e), 32), 32), :
+                        ],
+                        send_sem=grad_send,
+                        recv_sem=grad_recv,
+                        device_id=(host, chips[e]),
+                        device_id_type=MESH,
+                    ).start()
+
+                if e == 0 and side == 0:
+                    pl.when(d > 0)(go)
+                else:
+                    go()
+        return 0
+
+    lax.fori_loop(0, 8, send, 0)
+    rcv[0:32, :] = out[0:32, :]
+
+    def hop(a, stage, step, src, dst):
+        copy = pltpu.make_async_remote_copy(
+            src_ref=src,
+            dst_ref=dst,
+            send_sem=sum_send.at[a, stage, step - 1],
+            recv_sem=sum_recv.at[a, stage, step - 1],
+            device_id=shifted(me, AXES[a][stage], step),
+            device_id_type=MESH,
+        )
+        copy.start()
+        return copy
+
+    hops = []
+    for a in range(3):
+        pair[2 * a].wait_recv()
+        pair[2 * a + 1].wait_recv()
+
+        def product(j, _):
+            cols = pl.ds(pl.multiple_of(j * 512, 512), 512)
+            sums = jnp.dot(mine[a], wides[a][:, cols], preferred_element_type=jnp.float32)
+            sums = sums + jnp.dot(lefts[a], rights[a, :, cols], preferred_element_type=jnp.float32)
+            part[a, :, cols] = sums.astype(jnp.bfloat16)
+            return 0
+
+        lax.fori_loop(0, 7, product, 0)
+        hops.append(
+            [
+                hop(a, 0, step, part.at[a, pl.ds(64 * step, 64), :], first.at[a, step - 1])
+                for step in (2, 1, 3)
+            ]
+        )
+
+    whole = pl.ds(32, 4064)
+    pltpu.make_async_copy(rcv.at[whole, :], rcv.at[whole, :], grad_recv).wait()
+    inc = inc_ref[...]
+    inc_t = inc.T
+    for k in range(128):
+        g, c = k % 32, k // 32
+        half = jnp.broadcast_to(inc_t[0:32, k : k + 1] >> 11, (32, 128))
+        grad = rcv[32 * k : 32 * k + 32, :].astype(jnp.float32)
+        at = (g * 4 + c) * 32
+        spread[at : at + 32, 0:128] = jnp.where(half == 0, grad, 0.0).astype(jnp.bfloat16)
+        spread[at : at + 32, 128:256] = jnp.where(half == 1, grad, 0.0).astype(jnp.bfloat16)
+    asked = jnp.concatenate([inc[32 * c : 32 * c + 32, 0:32] for c in range(4)], axis=1) & 2047
+
+    def update(m, _):
+        at = pl.multiple_of(m * 256, 256)
+        row = lax.broadcasted_iota(jnp.int32, (256, 128), 0) + at
+        picks = jnp.concatenate([hot(row == asked[g : g + 1, :]) for g in range(32)], axis=1)
+        sums = jnp.dot(picks, spread[...], preferred_element_type=jnp.float32)
+        for side in range(2):
+            for block in range(2):
+                i = side * 16 + m * 2 + block
+                here = pl.ds(pl.multiple_of(i * 128, 128), 128)
+                row_grad = sums[128 * block : 128 * block + 128, 128 * side : 128 * side + 128]
+                acc = to_column(acc_ref[pl.ds(i, 1), :])
+                acc = acc + jnp.sum(row_grad * row_grad, axis=1, keepdims=True) * (1.0 / 128.0)
+                new_acc_ref[pl.ds(i, 1), :] = acc.T[0:1, :]
+                values = rows_ref[here, :].astype(jnp.float32) * to_column(scale_ref[pl.ds(i, 1), :])
+                values = values - LEARN_RATE * row_grad / jnp.sqrt(acc)
+                top = jnp.max(jnp.abs(values), axis=1, keepdims=True)
+                scale = (jnp.broadcast_to(top, (128, 128)) + 1e-06) / QUANT_TOP
+                new_scale_ref[pl.ds(i, 1), :] = scale.T[0:1, :]
+                new_rows_ref[here, :] = (values / scale).astype(jnp.bfloat16)
+        return 0
+
+    lax.fori_loop(0, 8, update, 0)
+
+    for a in range(3):
+        for copy in hops[a]:
+            copy.wait_recv()
+
+        def gather(j, _):
+            cols = pl.ds(pl.multiple_of(j * 512, 512), 512)
+            sums = part[a, 0:64, cols].astype(jnp.float32)
+            for step in range(3):
+                sums = sums + first[a, step, :, cols].astype(jnp.float32)
+            second_src[a, :, cols] = sums.astype(jnp.bfloat16)
+            return 0
+
+        lax.fori_loop(0, 7, gather, 0)
+        hops[a] = hops[a] + [
+            hop(a, 1, step, second_src.at[a, pl.ds(16 * step, 16), :], second.at[a, step - 1])
+            for step in (2, 1, 3)
+        ]
+    for a in range(3):
+        for copy in hops[a][3:]:
+            copy.wait_recv()
+        sums = second_src[a, 0:16, :].astype(jnp.float32)
+        for step in range(3):
+            sums = sums + second[a, step].astype(jnp.float32)
+        for step in range(4):
+            piece = sums[4 * step : 4 * step + 4, :]
+            third_src[a, step] = jnp.concatenate(
+                [piece[:, 896 * i : 896 * i + 896] for i in range(4)], axis=0
+            ).astype(jnp.bfloat16)
+        hops[a] = hops[a] + [
+            hop(a, 2, step, third_src.at[a, step], third.at[a, step - 1]) for step in (2, 1, 3)
+        ]
+    for a, out_ref in enumerate((out_down_ref, out_hid_ref, out_up_ref)):
+        for copy in hops[a][6:]:
+            copy.wait_recv()
+        sums = third_src[a, 0].astype(jnp.float32)
+        for step in range(3):
+            sums = sums + third[a, step].astype(jnp.float32)
+        sums = sums * (1.0 / 128.0)
+        sums = jnp.concatenate([sums[4 * i : 4 * i + 4, :] for i in range(4)], axis=1)
+        out_ref[...] = sums[:, 0:3341]
+
+    for copy in pair + hops[0] + hops[1] + hops[2]:
+        copy.wait_send()
+    pltpu.make_async_copy(out.at[whole, :], out.at[whole, :], grad_send).wait()
+
+
+def update(*operands):
+    vmem = pl.BlockSpec(memory_space=pltpu.VMEM)
+    bf16, f32 = jnp.bfloat16, jnp.float32
+    dense_out = jax.ShapeDtypeStruct((4, 3341), f32)
+    return pl.pallas_call(
+        update_kernel,
+        name="update",
+        out_shape=(
+            jax.ShapeDtypeStruct((4096, 128), bf16),
+            jax.ShapeDtypeStruct((32, 128), f32),
+            jax.ShapeDtypeStruct((32, 128), f32),
+            jax.ShapeDtypeStruct((2048, 128), f32),
+            dense_out,
+            dense_out,
+            dense_out,
+        ),
+        in_specs=[vmem] * 14,
+        out_specs=(vmem,) * 7,
+        scratch_shapes=[
+            pltpu.VMEM((6656, 256), bf16),
+            pltpu.VMEM((2048, 256), bf16),
+            pltpu.VMEM((4096, 128), bf16),
+            pltpu.VMEM((4096, 128), bf16),
+            pltpu.VMEM((4096, 256), bf16),
+            pltpu.VMEM((3, 256, 256), bf16),
+            pltpu.VMEM((3, 256, 256), bf16),
+            pltpu.VMEM((3, 256, 256), bf16),
+            pltpu.VMEM((3, 256, 3584), bf16),
+            pltpu.VMEM((3, 256, 3584), bf16),
+            pltpu.VMEM((3, 3, 64, 3584), bf16),
+            pltpu.VMEM((3, 64, 3584), bf16),
+            pltpu.VMEM((3, 3, 16, 3584), bf16),
+            pltpu.VMEM((3, 4, 16, 896), bf16),
+            pltpu.VMEM((3, 3, 16, 896), bf16),
+            pltpu.SemaphoreType.DMA((3, 2)),
+            pltpu.SemaphoreType.DMA((3, 2)),
+            pltpu.SemaphoreType.DMA,
+            pltpu.SemaphoreType.DMA,
+            pltpu.SemaphoreType.DMA((3, 3, 3)),
+            pltpu.SemaphoreType.DMA((3, 3, 3)),
+        ],
+        compiler_params=pltpu.CompilerParams(
+            collective_id=1, has_side_effects=True, vmem_limit_bytes=56 * 2**20
+        ),
+    )(*operands)
 
 
 def on_device(
@@ -351,64 +743,54 @@
     hidden_bias,
     out_weight,
 ):
-    n_host = lax.axis_size("hst")
-    n_chip = lax.axis_size("chip")
-    devices = n_host * n_chip
-    owners = needed_owner[:, 0]
-    need_rows = owners.shape[0]
-    capacity = 2 * need_rows // devices
-    emb_width = table_rows.shape[1]
-    batch_rows = dense_feats.shape[0]
-    owner_hits = (owners[:, None] == jnp.arange(devices, dtype=jnp.int32)[None, :]).astype(
-        jnp.int32
-    )
-    places = jnp.sum(jnp.cumsum(owner_hits, axis=0) * owner_hits, axis=1) - 1
-    requests = jnp.full((devices, capacity), -1, jnp.int32).at[owners, places].set(needed_local)
-    incoming = send_requests(requests)
-    row_index = jnp.where(incoming >= 0, incoming, 0)
-    embedded, _, _ = embed(
-        owners.reshape(1, -1),
-        needed_local.reshape(1, -1),
-        slot_ids.T,
+    slots_t = slot_ids.T
+    up_t = cross_up.T
+    scale = table_scale.reshape(32, 128)
+    base, pos, asked = embed(
+        needed_owner.reshape(1, 2048),
+        needed_local.reshape(1, 2048),
+        slots_t,
         table_rows,
-        table_scale.reshape(32, 128),
-    )
-    base_in = jnp.concatenate([embedded, dense_feats], axis=1)
-    low_rank, crossed, grad_hidden, grad_mix, grad_low, grad_input = dense_step(
-        base_in, labels, cross_down, cross_up, cross_bias, hidden_weight, hidden_bias, out_weight
-    )
-    emb_cols = embedded.shape[1]
-    emb_grad = grad_input[:, :emb_cols].reshape(-1, emb_width)
-    slot_grad = jax.ops.segment_sum(emb_grad, slot_ids.reshape(-1), num_segments=need_rows)
-    evict_wide = evicted.astype(jnp.float32)[:, None]
-    cache_grad = slot_grad * (1.0 - evict_wide)
-    outgoing = (
-        jnp.zeros((devices, capacity, emb_width), jnp.float32)
-        .at[owners, places]
-        .set(slot_grad * evict_wide)
-    )
-    received = send_grads(outgoing)
-    row_grad = jax.ops.segment_sum(
-        received.reshape(-1, emb_width), row_index.reshape(-1), num_segments=table_rows.shape[0]
-    )
-    new_accum = table_acc + jnp.mean(row_grad * row_grad, axis=1)
-    values = (
-        table_rows.astype(jnp.float32) * table_scale[:, None]
-        - LEARN_RATE * row_grad / jnp.sqrt(new_accum)[:, None]
-    )
-    new_scale = (jnp.max(jnp.abs(values), axis=1) + 1e-06) / QUANT_TOP
-    new_rows = (values / new_scale[:, None]).astype(jnp.bfloat16)
-    partials = (
-        contract_first(grad_low, base_in) / devices,
-        contract_first(grad_hidden, crossed) / devices,
-        contract_first(low_rank, grad_mix) / devices,
-    )
-    grad_down, grad_hid, grad_up = (
-        lax.psum_scatter(partials[0], ("hst", "chip"), scatter_dimension=0, tiled=True),
-        lax.psum_scatter(partials[1], ("hst", "chip"), scatter_dimension=0, tiled=True),
-        lax.psum_scatter(partials[2], ("hst", "chip"), scatter_dimension=0, tiled=True),
-    )
-    return (new_rows, new_scale, new_accum, cache_grad, grad_down, grad_hid, grad_up)
+        scale,
+        jnp.pad(dense_feats, ((0, 0), (0, 243))),
+    )
+    tails = jnp.concatenate([cross_down[3328:], up_t[3328:], hidden_weight[3328:]], axis=1)
+    grad, crossed, mix, low, grad_hid, grad_low = dense(
+        base,
+        labels.astype(jnp.float32).reshape(1, 256),
+        cross_down,
+        up_t,
+        hidden_weight,
+        jnp.pad(tails, ((0, 243), (0, 0))),
+        jnp.pad(cross_bias, (0, 243)).reshape(1, 3584),
+        hidden_bias.reshape(1, 512),
+        out_weight.astype(jnp.float32).reshape(1, 512),
+    )
+    new_rows, new_scale, new_acc, cache, grad_down, grad_hidden, grad_up = update(
+        grad,
+        base,
+        crossed,
+        mix,
+        low,
+        grad_hid,
+        grad_low,
+        pos.reshape(16, 128),
+        asked,
+        slots_t,
+        evicted.reshape(16, 128),
+        table_rows,
+        scale,
+        table_acc.reshape(32, 128),
+    )
+    return (
+        new_rows,
+        new_scale.reshape(4096),
+        new_acc.reshape(4096),
+        cache,
+        grad_down,
+        grad_hidden,
+        grad_up,
+    )
 
 
 def solution(mesh):

time: 340 us -> 154 us (0.45)
  waiting for transfers between devices: 124 us -> 0 us
  Pallas kernels: 48.3 us -> 131 us
  other arithmetic: 82 us -> 1.5 us
  matrix products: 24 us -> 0 us
  starting transfers between devices: 16.8 us -> 0 us
  between operations: 14.5 us -> 0.8 us
  local copies, waits for them, and re-layouts: 28.3 us -> 18.9 us
    unnamed x2 -> x0, waiting for transfers between devices: 97 us -> none
    pallas_call x0 -> x2, Pallas kernels: none -> 83.5 us  [the longest x1 64.5 us: update(): pl.pallas_call(update_kernel, name='update', out_shape=(jax.ShapeDtypeStr...]
    scatter-add x2 -> x0, other arithmetic: 61.4 us -> none  [the longest x1 36.5 us: on_device(): jax.ops.segment_sum(emb_grad, slot_ids.reshape(-1), num_segments=need_rows)]
    all_to_all x2 -> x0, waiting for transfers between devices: 27 us -> none  [the longest x1 27 us: send_grads(): lax.all_to_all(outgoing, ('hst', 'chip'), split_axis=0, concat_axis=0, ti...]
    dot_general x10 -> x0, matrix products: 24 us -> none  [the longest x3 12.4 us: contract_first(): lax.dot_general(left, right, (((0,), (0,)), ((), ())), preferred_element_...]
    all_to_all x2 -> x0, starting transfers between devices: 16.7 us -> none  [the longest x1 9.73 us: send_grads(): lax.all_to_all(outgoing, ('hst', 'chip'), split_axis=0, concat_axis=0, ti...]
    unnamed x4 -> x0, other arithmetic: 8.28 us -> none
    unnamed x58 -> x48, local copies, waits for them, and re-layouts: 21.8 us -> 16 us
  transfers between devices with their start and end apart: 3 -> 0, of which waited for: 2 -> 0; matrix products, arithmetic and copies ran while one was open for 29% -> 0% of each run, Pallas kernels for 0% -> 0%
where the time goes in v2:
time: 154 us; the launch traced here: 152 us
  Pallas kernels  131 us (85%)
  local copies, waits for them, and re-layouts  18.9 us (12%)
    pallas_call x1, Pallas kernels, update(): pl.pallas_call(update_kernel, name='update', out_shape=(jax.ShapeDtypeStr...  64.5 us
    pallas_call x1, Pallas kernels, embed(): pl.pallas_call(embed_kernel, name='embed', out_shape=(jax.ShapeDtypeStruc...  47.5 us
    pallas_call x1, Pallas kernels, dense(): pl.pallas_call(dense_kernel, name='dense', out_shape=(jax.ShapeDtypeStruc...  18.9 us
    unnamed x48, local copies, waits for them, and re-layouts  16 us

profile of v2, /device:TPU:6, one launch (start us, length us, event | category | flops | bytes accessed | tf_op | source)
XLA Modules:
  0.0 152.1 jit_solution(6027861839217907680)
XLA Ops:
  0.6 0.0 copy-start
  0.6 0.0 copy-start.13
  0.7 0.8 convert_element_type.10
  1.4 0.7 reshape.65
  2.1 0.7 slice.12
  2.8 0.7 pad.14
  3.6 0.7 slice.9
  4.3 0.7 slice.11
  5.0 0.8 copy.22
  5.9 0.1 fusion.4.tails_ref
  5.9 0.0 copy-done
  5.9 0.0 copy-start.7
  5.9 0.7 copy-done.7
  6.7 0.0 copy-start.9
  6.7 0.7 copy-done.9
  7.4 0.0 copy-start.10
  7.4 0.7 copy-done.10
  8.1 0.0 copy-start.11
  8.1 0.7 copy-done.11
  8.8 47.5 %embed.1 = (bf16[256,3584]{1,0:T(8,128)(2,1)S(1)}, s32[1,2048]{1,0:T(1,128)S(1)}, s32[128,128]{1,0:T(8,128)S(1)}) custom-call(s32[1,2048]{1,0:T(1,128)S(1)} %bitcast.17, s32[1,2048]{1,0:T(1,128)S(1)} %bitcast.18, s32[26,256]{1,0:T(8,128)S(1)} %bitcast.14, bf16[4096,128]{1,0:T(8,128)(2,1)S(1)} %copy-done, f32[32,128]{1,0:T(8,128)S(1)} %bitcast.16, ...), custom_call_target="tpu_custom_call" | custom-call | tf_op jit(solution)/shard_map/embed/pallas_call | solution.py:268
  56.3 0.0 copy-start.1
  56.3 1.3 copy-done.1
  57.5 0.0 copy-start.8
  57.6 0.0 copy-start.12
  57.6 0.0 copy-done.13
  57.6 18.9 %dense.1 = (bf16[256,3328]{1,0:T(8,128)(2,1)S(1)}, bf16[256,3584]{1,0:T(8,128)(2,1)S(1)}, bf16[256,3584]{1,0:T(8,128)(2,1)}, bf16[256,512]{1,0:T(8,128)(2,1)S(1)...) custom-call(bf16[256,3584]{1,0:T(8,128)(2,1)} %copy-done.1, f32[1,256]{1,0:T(1,128)S(1)} %bitcast.21, ...), custom_call_target="tpu_custom_call" | custom-call | flops 5637144576 | bytes 18874368 | tf_op jit(solution)/shard_map/dense/pallas_call | solution.py:390
  76.5 0.0 copy-done.8
  76.5 0.0 copy-done.12
  76.5 0.0 copy-start.2
  76.5 1.2 copy-done.2
  77.8 0.0 copy-start.3
  77.8 1.2 copy-done.3
  79.0 0.0 copy-start.4
  79.0 0.7 copy-done.4
  79.7 0.0 copy-start.5
  79.7 0.7 copy-done.5
  80.4 0.0 copy-start.6
  80.4 0.7 copy-done.6
  81.1 64.5 %update.1 = (bf16[4096,128]{1,0:T(8,128)(2,1)}, f32[32,128]{1,0:T(8,128)}, f32[32,128]{1,0:T(8,128)}, f32[2048,128]{1,0:T(8,128)}, f32[4,3341]{1,0:T(4,128)}, /*index=5*/f32[4,3341]{1,0:T(4,128)}, f32[4,3341]{1,0:T(4,128)}) custom-call(bf16[256,3328]{1,0:T(8,128)(2,1)} %copy-done.3, bf16[256,3584]{1,0:T(8,128)(2,1)} %copy-done.1, ...), custom_call_target="tpu_custom_call" | custom-call | tf_op jit(solution)/shard_map/update/pallas_call | solution.py:686
  145.7 0.0 copy-start.19
  145.7 0.0 copy-start.18
  145.7 0.0 copy-start.14
  145.7 0.0 copy-start.17
  145.7 0.0 copy-start.16
  145.7 2.3 %copy.30 = bf16[4096,128]{1,0:T(8,128)(2,1)} copy(bf16[4096,128]{1,0:T(8,128)(2,1)} %get-tuple-element.46) | data formatting | bytes 2097152
  148.1 0.0 copy-done.19
  148.1 0.0 copy-start.15
  148.1 0.6 copy.31
  148.7 0.0 copy-done.18
  148.7 0.6 copy.32
  149.3 0.0 copy-done.14
  149.3 1.0 copy.33
  150.3 0.0 copy-done.17
  150.3 0.6 copy.34
  150.9 0.0 copy-done.16
  150.9 0.6 copy.35
  151.5 0.0 copy-done.15
  151.5 0.6 copy.36
  (2 shorter events, 0.0 us)
Async XLA Ops:
  0.6 5.3 %copy-start = (bf16[4096,128]{1,0:T(8,128)(2,1)S(1)}, bf16[4096,128]{1,0:T(8,128)(2,1)}, u32[]{:S(2)}) copy-start(bf16[4096,128]{1,0:T(8,128)(2,1)} %rows_ref.3) | copy-start | bytes 3145732
  0.6 56.9 %copy-start.13 = (f32[512]{0:T(512)S(1)}, f32[512]{0:T(512)}, u32[]{:S(2)}) copy-start(f32[512]{0:T(512)} %param.28) | copy-start | bytes 6148
  5.9 0.8 copy-start.7
  6.7 0.7 copy-start.9
  7.4 0.7 copy-start.10
  8.1 0.7 copy-start.11
  56.3 1.3 copy-start.1
  57.5 19.0 %copy-start.8 = (s32[128,128]{1,0:T(8,128)}, s32[128,128]{1,0:T(8,128)S(1)}, u32[]{:S(2)}) copy-start(s32[128,128]{1,0:T(8,128)S(1)} %get-tuple-element.31.inc_ref) | copy-start | bytes 196612
  57.6 19.0 %copy-start.12 = (s32[1,2048]{1,0:T(1,128)}, s32[1,2048]{1,0:T(1,128)S(1)}, u32[]{:S(2)}) copy-start(s32[1,2048]{1,0:T(1,128)S(1)} %get-tuple-element.30) | copy-start | bytes 24580
  76.5 1.3 copy-start.2
  77.8 1.2 copy-start.3
  79.0 0.7 copy-start.4
  79.7 0.7 copy-start.5
  80.4 0.7 copy-start.6
  145.7 2.4 %copy-start.19 = (f32[32,128]{1,0:T(8,128)S(1)}, f32[32,128]{1,0:T(8,128)}, u32[]{:S(2)}) copy-start(f32[32,128]{1,0:T(8,128)} %get-tuple-element.33) | copy-start | bytes 49156
  145.7 3.0 %copy-start.18 = (f32[32,128]{1,0:T(8,128)S(1)}, f32[32,128]{1,0:T(8,128)}, u32[]{:S(2)}) copy-start(f32[32,128]{1,0:T(8,128)} %get-tuple-element.34) | copy-start | bytes 49156
  145.7 3.6 %copy-start.14 = (f32[2048,128]{1,0:T(8,128)S(1)}, f32[2048,128]{1,0:T(8,128)}, u32[]{:S(2)}) copy-start(f32[2048,128]{1,0:T(8,128)} %get-tuple-element.49) | copy-start | bytes 3145732
  145.7 4.6 %copy-start.17 = (f32[4,3341]{1,0:T(4,128)S(1)}, f32[4,3341]{1,0:T(4,128)}, u32[]{:S(2)}) copy-start(f32[4,3341]{1,0:T(4,128)} %get-tuple-element.50) | copy-start | bytes 160372
  145.7 5.2 %copy-start.16 = (f32[4,3341]{1,0:T(4,128)S(1)}, f32[4,3341]{1,0:T(4,128)}, u32[]{:S(2)}) copy-start(f32[4,3341]{1,0:T(4,128)} %get-tuple-element.51) | copy-start | bytes 160372
  148.1 3.4 %copy-start.15 = (f32[4,3341]{1,0:T(4,128)S(1)}, f32[4,3341]{1,0:T(4,128)}, u32[]{:S(2)}) copy-start(f32[4,3341]{1,0:T(4,128)} %get-tuple-element.52) | copy-start | bytes 160372

commit v3 on v1

v3 whole, which is shorter than its diff:
```python
import functools

import jax
import jax.experimental.pallas as pl
import jax.experimental.pallas.tpu as pltpu
import jax.numpy as jnp
from jax import lax
from jax.sharding import PartitionSpec as P

MESH = pl.DeviceIdType.MESH
LEARN_RATE = 0.1
QUANT_TOP = 4.0


def contract_last(left, right):
    return lax.dot_general(
        left, right, (((1,), (1,)), ((), ())), preferred_element_type=jnp.float32
    )


def contract_first(left, right):
    return lax.dot_general(
        left, right, (((0,), (0,)), ((), ())), preferred_element_type=jnp.float32
    )


def coords():
    host = lax.axis_index("hst")
    chip = lax.axis_index("chip")
    return host // 4, host % 4, chip // 2, chip % 2


def hosts_from(y, z):
    return [((y + d // 4) % 4) * 4 + (z + d % 4) % 4 for d in range(16)]


def chips_from(x, core):
    return [((x + d // 2) % 4) * 2 + (core + d % 2) % 2 for d in range(8)]


def neg_host(d):
    return ((4 - d // 4) % 4) * 4 + (4 - d % 4) % 4


def neg_chip(d):
    return ((4 - d // 2) % 4) * 2 + d % 2


def greet_all(barrier):
    y, z, x, core = coords()
    chips = chips_from(x, core)

    def one(d, _):
        host = ((y + d // 4) % 4) * 4 + (z + d % 4) % 4
        for e in range(8):
            if e == 0:

                @pl.when(d > 0)
                def _():
                    pl.semaphore_signal(barrier, inc=1, device_id=(host, chips[0]), device_id_type=MESH)

            else:
                pl.semaphore_signal(barrier, inc=1, device_id=(host, chips[e]), device_id_type=MESH)
        return 0

    lax.fori_loop(0, 16, one, 0)


def hot(cond):
    return jnp.where(cond, 1.0, 0.0).astype(jnp.bfloat16)


def to_column(row):
    return jnp.broadcast_to(row, (128, 128)).T


def lane_tiles(col, count):
    lane = lax.broadcasted_iota(jnp.int32, col.shape, 1)
    return jnp.concatenate([hot(col == lane + 128 * i) for i in range(count)], axis=1)


AXES = (("y", "z", "x"), ("z", "x", "y"), ("x", "y", "z"))
DOWN, UP, HID = 0, 1, 2


def row_order(array, me):
    row = lax.broadcasted_iota(jnp.int32, (512, 512), 0)
    at = {"core": (me["core"] + (row >> 8)) & 1}
    for stage, axis in enumerate(AXES[array]):
        at[axis] = (me[axis] + (row >> (6 - 2 * stage))) & 3
    source = (at["y"] * 32 + at["z"] * 8 + at["x"] * 2 + at["core"]) * 4 + (row & 3)
    return hot(source == lax.broadcasted_iota(jnp.int32, (512, 512), 1))


def shifted(me, axis, step):
    to = dict(me)
    to[axis] = (me[axis] + step) % 4
    return (to["y"] * 4 + to["z"], to["x"] * 2 + to["core"])


def step_kernel(
    owner_ref,
    local_ref,
    slots_ref,
    feats_ref,
    labels_ref,
    evict_ref,
    rows_hbm,
    scale_ref,
    acc_ref,
    down_hbm,
    up_hbm,
    hid_hbm,
    down_tail,
    up_tail,
    hid_tail,
    bias_ref,
    hid_bias_ref,
    out_w_ref,
    new_rows_hbm,
    new_scale_ref,
    new_acc_ref,
    cache_hbm,
    out_down_ref,
    out_hid_ref,
    out_up_ref,
    rows_ref,
    new_rows_ref,
    cache_ref,
    weights,
    bias,
    req,
    inc,
    asked_ref,
    val,
    ret,
    rcv,
    table2,
    qcol,
    pos,
    poscol,
    fetched,
    fetched2,
    factor,
    wides,
    rights,
    low_ref,
    grad_hid_ref,
    grad_low_ref,
    split,
    placed,
    spread,
    mine,
    theirs,
    lefts,
    first,
    second_src,
    second,
    third_src,
    third,
    load_sems,
    side_sems,
    req_send,
    req_recv,
    val_send,
    val_recv,
    pair_send,
    pair_recv,
    grad_send,
    grad_recv,
    sum_send,
    sum_recv,
):
    y, z, x, core = coords()
    me = {"y": y, "z": z, "x": x, "core": core}
    chips = chips_from(x, core)
    partner = (y * 4 + z, x * 2 + 1 - core)
    barrier = pltpu.get_barrier_semaphore()
    greet_all(barrier)
    base, crossed, mix = wides.at[0], wides.at[1], wides.at[2]

    rows_load = pltpu.make_async_copy(rows_hbm, rows_ref, side_sems.at[0])
    rows_load.start()
    loads = []
    for i, src in enumerate((down_hbm, up_hbm, hid_hbm)):
        some = []
        for j in range(13):
            copy = pltpu.make_async_copy(
                src.at[pl.ds(256 * j, 256), :], weights.at[i, j], load_sems.at[i, j]
            )
            copy.start()
            some.append(copy)
        loads.append(some)

    owner = owner_ref[...]
    rel = (
        (((owner >> 5) - y) & 3) * 32
        + (((owner >> 3) - z) & 3) * 8
        + (((owner >> 1) - x) & 3) * 2
        + ((owner - core) & 1)
    )
    sub = lax.broadcasted_iota(jnp.int32, (128, 256), 0)
    upper = hot(
        lax.broadcasted_iota(jnp.int32, (256, 256), 0)
        < lax.broadcasted_iota(jnp.int32, (256, 256), 1)
    )
    seen = jnp.zeros((128, 1), jnp.float32)
    hi_sum = jnp.zeros((128, 32), jnp.float32)
    lo_sum = jnp.zeros((128, 32), jnp.float32)
    for i in range(8):
        part = rel[:, 256 * i : 256 * i + 256]
        hits = hot(part == sub)
        before = jnp.dot(hits, upper, preferred_element_type=jnp.float32) + seen
        wide = hits.astype(jnp.float32)
        place = jnp.sum(wide * before, axis=0, keepdims=True).astype(jnp.int32)
        seen = seen + jnp.sum(wide, axis=1, keepdims=True)
        where = part * 32 + place
        pos[2 * i : 2 * i + 1, :] = where[:, 0:128]
        pos[2 * i + 1 : 2 * i + 2, :] = where[:, 128:256]
        code = local_ref[:, 256 * i : 256 * i + 256] + 1
        here = place == lax.broadcasted_iota(jnp.int32, (32, 256), 0)
        hi = jnp.where(here, (code >> 6).astype(jnp.float32), 0.0).astype(jnp.bfloat16)
        lo = jnp.where(here, (code & 63).astype(jnp.float32), 0.0).astype(jnp.bfloat16)
        hi_sum = hi_sum + contract_last(hits, hi)
        lo_sum = lo_sum + contract_last(hits, lo)
    asked = (hi_sum * 64.0 + lo_sum).astype(jnp.int32) - 1
    asked = jnp.concatenate([asked, jnp.full((128, 96), -1, jnp.int32)], axis=1)
    for k in range(128):
        req[k] = asked[k : k + 1, :]
    inc[0] = req[0]

    pl.semaphore_wait(barrier, 127)

    def ask(d, _):
        host = ((y + d // 4) % 4) * 4 + (z + d % 4) % 4
        back = ((4 - d // 4) % 4) * 4 + (4 - d % 4) % 4
        for e in range(8):

            def go():
                pltpu.make_async_remote_copy(
                    src_ref=req.at[d * 8 + e],
                    dst_ref=inc.at[back * 8 + neg_chip(e)],
                    send_sem=req_send,
                    recv_sem=req_recv,
                    device_id=(host, chips[e]),
                    device_id_type=MESH,
                ).start()

            if e == 0:
                pl.when(d > 0)(go)
            else:
                go()
        return 0

    lax.fori_loop(0, 16, ask, 0)

    rows_load.wait()
    for i in range(32):
        rows = rows_ref[128 * i : 128 * i + 128, :].astype(jnp.float32)
        col = to_column(scale_ref[i : i + 1, :])
        table2[
            (i % 8) * 128 : (i % 8) * 128 + 128, (i // 8) * 128 : (i // 8) * 128 + 128
        ] = (rows * col).astype(jnp.bfloat16)
    for i in range(16):
        poscol[128 * i : 128 * i + 128, :] = to_column(pos[i : i + 1, :])
    ids = jnp.concatenate([slots_ref[...], jnp.zeros((102, 256), jnp.int32)], axis=0).T
    ids = ids.astype(jnp.float32)
    for t in range(26):
        factor[t] = jnp.broadcast_to(ids[:, t : t + 1], (256, 128))
    feats = jnp.concatenate(
        [feats_ref[...].astype(jnp.float32), jnp.zeros((115, 256), jnp.float32)], axis=0
    )
    base[:, 3328:3456] = feats.T.astype(jnp.bfloat16)
    base[:, 3456:3584] = jnp.zeros((256, 128), jnp.bfloat16)
    bias[...] = jnp.zeros((1, 3584), jnp.float32)
    bias[:, 0:3341] = bias_ref[...].reshape(1, 3341)
    inside = lax.broadcasted_iota(jnp.int32, (128, 512), 0) < 13
    for i, tail in enumerate((down_tail, up_tail, hid_tail)):
        weights[i, 13, 0:128, :] = jnp.where(inside, tail[...].astype(jnp.float32), 0.0).astype(
            jnp.bfloat16
        )
        weights[i, 13, 128:256, :] = jnp.zeros((128, 512), jnp.bfloat16)

    pltpu.make_async_copy(req.at[pl.ds(0, 127)], req.at[pl.ds(0, 127)], req_send).wait()
    pltpu.make_async_copy(inc.at[pl.ds(1, 127)], inc.at[pl.ds(1, 127)], req_recv).wait()
    got = inc[...].reshape(128, 128)
    asked_ref[...] = got
    got_t = got.T
    for k in range(128):
        qcol[32 * k : 32 * k + 32, :] = jnp.broadcast_to(got_t[0:32, k : k + 1], (32, 128))

    def send_blocks(d, skip_self, src, dst, send_sem, recv_sem):
        start = pl.multiple_of(d * 256, 256)
        host = ((y + d // 4) % 4) * 4 + (z + d % 4) % 4
        back = ((4 - d // 4) % 4) * 4 + (4 - d % 4) % 4
        for e in range(8):

            def go():
                pltpu.make_async_remote_copy(
                    src_ref=src.at[pl.ds(pl.multiple_of(start + 32 * e, 32), 32), :],
                    dst_ref=dst.at[pl.ds(pl.multiple_of(back * 256 + 32 * neg_chip(e), 32), 32), :],
                    send_sem=send_sem,
                    recv_sem=recv_sem(back // 4),
                    device_id=(host, chips[e]),
                    device_id_type=MESH,
                ).start()

            if e == 0 and skip_self:
                pl.when(d > 0)(go)
            else:
                go()

    def serve(i, _):
        at = pl.multiple_of(i * 512, 512)
        query = qcol[pl.ds(at, 512), :]
        found = jnp.dot(
            lane_tiles(query & 1023, 8), table2[...], preferred_element_type=jnp.float32
        )
        quarter = query >> 10
        result = jnp.zeros((512, 128), jnp.float32)
        for q in range(4):
            result = jnp.where(quarter == q, found[:, 128 * q : 128 * q + 128], result)
        val[pl.ds(at, 512), :] = result.astype(jnp.bfloat16)
        send_blocks(2 * i, True, val, ret, val_send, lambda c: val_recv.at[c])
        send_blocks(2 * i + 1, False, val, ret, val_send, lambda c: val_recv.at[c])
        return 0

    lax.fori_loop(0, 8, serve, 0)
    ret[0:32, :] = val[0:32, :]
    for chunk in (0, 3, 2, 1):
        if chunk == 0:
            landed = ret.at[pl.ds(32, 992), :]
        else:
            landed = ret.at[pl.ds(1024 * chunk, 1024), :]
        pltpu.make_async_copy(landed, landed, val_recv.at[chunk]).wait()
        sides = jnp.concatenate(
            [
                ret[1024 * chunk : 1024 * chunk + 512, :],
                ret[1024 * chunk + 512 : 1024 * chunk + 1024, :],
            ],
            axis=1,
        )

        def pick(i, _):
            at = pl.multiple_of(i * 512, 512)
            where = poscol[pl.ds(at, 512), :]
            found = jnp.dot(lane_tiles(where & 511, 4), sides, preferred_element_type=jnp.float32)
            half = where >> 9
            if chunk == 0:
                result = jnp.zeros((512, 128), jnp.float32)
            else:
                result = fetched[pl.ds(at, 512), :]
            result = jnp.where(half == 2 * chunk, found[:, :128], result)
            fetched[pl.ds(at, 512), :] = jnp.where(half == 2 * chunk + 1, found[:, 128:], result)
            return 0

        lax.fori_loop(0, 4, pick, 0)
    fetched2[:, 0:128] = fetched[0:1024, :].astype(jnp.bfloat16)
    fetched2[:, 128:256] = fetched[1024:2048, :].astype(jnp.bfloat16)

    def fill(i, _):
        slot = factor[pl.ds(2 * i, 2)].reshape(512, 128).astype(jnp.int32)
        found = jnp.dot(
            lane_tiles(slot & 1023, 8), fetched2[...], preferred_element_type=jnp.float32
        )
        result = jnp.where(slot < 1024, found[:, :128], found[:, 128:]).astype(jnp.bfloat16)
        base[:, pl.ds(pl.multiple_of(256 * i, 128), 128)] = result[0:256]
        base[:, pl.ds(pl.multiple_of(256 * i + 128, 128), 128)] = result[256:512]
        return 0

    lax.fori_loop(0, 13, fill, 0)

    def give(array, side, src, dst):
        copy = pltpu.make_async_remote_copy(
            src_ref=src,
            dst_ref=dst,
            send_sem=pair_send.at[array, side],
            recv_sem=pair_recv.at[array, side],
            device_id=partner,
            device_id_type=MESH,
        )
        copy.start()
        return copy

    def ordered(array, values):
        order = row_order(array, me)
        mine[array] = contract_last(order[0:256], values).astype(jnp.bfloat16)
        theirs[array] = contract_last(order[256:512], values).astype(jnp.bfloat16)
        return give(array, 0, theirs.at[array], lefts.at[array])

    pair = [give(0, 1, base, rights.at[0])]
    for copy in loads[DOWN]:
        copy.wait()
    low = jnp.dot(
        base[...], weights[DOWN].reshape(3584, 512), preferred_element_type=jnp.float32
    ).astype(jnp.bfloat16)
    low_ref[...] = low
    for copy in loads[UP]:
        copy.wait()

    def cross(j, _):
        cols = pl.ds(pl.multiple_of(j * 256, 256), 256)
        mixing = contract_last(low_ref[...], weights[UP, j]) + bias[:, cols]
        wide = base[:, cols].astype(jnp.float32)
        crossed[:, cols] = (wide * mixing + wide).astype(jnp.bfloat16)
        factor[2 * j] = mixing[:, 0:128] + 1.0
        factor[2 * j + 1] = mixing[:, 128:256] + 1.0
        return 0

    lax.fori_loop(0, 14, cross, 0)
    pair.append(give(1, 1, crossed, rights.at[1]))
    pair.append(ordered(2, low_ref[...]))
    for copy in loads[HID]:
        copy.wait()
    preact = (
        jnp.dot(
            crossed[...], weights[HID].reshape(3584, 512), preferred_element_type=jnp.float32
        )
        + hid_bias_ref[...]
    )
    sig = jax.nn.sigmoid(preact)
    hidden = (preact * sig).astype(jnp.bfloat16).astype(jnp.float32)
    out_w = out_w_ref[...].astype(jnp.float32).reshape(1, 512)
    logits = jnp.sum(hidden * out_w, axis=1, keepdims=True)
    labels = labels_ref[...].astype(jnp.float32)
    labels = jnp.concatenate([to_column(labels[:, 0:128]), to_column(labels[:, 128:256])], axis=0)
    grad_logit = jax.nn.sigmoid(logits) - labels[:, 0:1]
    grad_hid_ref[...] = (grad_logit * out_w * (sig * (1.0 + preact * (1.0 - sig)))).astype(
        jnp.bfloat16
    )
    pair.append(ordered(1, grad_hid_ref[...]))

    def back(j, _):
        cols = pl.ds(pl.multiple_of(j * 256, 256), 256)
        grad_cross = contract_last(grad_hid_ref[...], weights[HID, j])
        mix[:, cols] = (grad_cross * base[:, cols].astype(jnp.float32)).astype(jnp.bfloat16)
        factor[2 * j] = grad_cross[:, 0:128] * factor[2 * j]
        factor[2 * j + 1] = grad_cross[:, 128:256] * factor[2 * j + 1]
        return 0

    lax.fori_loop(0, 14, back, 0)
    pair.append(give(2, 1, mix, rights.at[2]))
    grad_low_ref[...] = jnp.dot(
        mix[...], weights[UP].reshape(3584, 512), preferred_element_type=jnp.float32
    ).astype(jnp.bfloat16)
    pair.append(ordered(0, grad_low_ref[...]))

    room = ((UP, 0), (HID, 0), (HID, 7))

    def hop(a, stage, step, src, dst):
        copy = pltpu.make_async_remote_copy(
            src_ref=src,
            dst_ref=dst,
            send_sem=sum_send.at[a, stage, step - 1],
            recv_sem=sum_recv.at[a, stage, step - 1],
            device_id=shifted(me, AXES[a][stage], step),
            device_id_type=MESH,
        )
        copy.start()
        return copy

    hops = [[], [], []]

    def multiply(a):
        place, at = room[a]

        def product(j, _):
            cols = pl.ds(pl.multiple_of(j * 512, 512), 512)
            both = jnp.concatenate([mine[a], lefts[a]], axis=1)
            wide = jnp.concatenate([wides[a, :, cols], rights[a, :, cols]], axis=0)
            weights[place, at + j] = jnp.dot(both, wide, preferred_element_type=jnp.float32).astype(
                jnp.bfloat16
            )
            return 0

        lax.fori_loop(0, 7, product, 0)
        for step in (2, 1, 3):
            src = weights.at[place, pl.ds(at, 7), pl.ds(64 * step, 64), :]
            hops[a].append(hop(a, 0, step, src, first.at[a, step - 1]))

    pair[1].wait_recv()
    pair[3].wait_recv()
    multiply(1)
    pair[2].wait_recv()
    pair[4].wait_recv()
    multiply(2)

    def last(j, _):
        grad = contract_last(grad_low_ref[...], weights[DOWN, j])
        for side in range(2):
            t = 2 * j + side
            wide = grad[:, 128 * side : 128 * side + 128] + factor[t]
            here = pl.ds(pl.multiple_of(t * 256, 256), 256)
            split[here, :] = jnp.concatenate([wide, wide], axis=1).astype(jnp.bfloat16)
        return 0

    lax.fori_loop(0, 13, last, 0)
    pair[0].wait_recv()
    pair[5].wait_recv()
    multiply(0)
    ids = jnp.concatenate([slots_ref[...], jnp.zeros((102, 256), jnp.int32)], axis=0).T
    for t in range(26):
        half = jnp.broadcast_to(ids[:, t : t + 1] >> 10, (256, 128))
        low_side = split[256 * t : 256 * t + 256, 0:128].astype(jnp.float32)
        split[256 * t : 256 * t + 256, 0:128] = jnp.where(half == 0, low_side, 0.0).astype(
            jnp.bfloat16
        )
        split[256 * t : 256 * t + 256, 128:256] = jnp.where(half == 1, low_side, 0.0).astype(
            jnp.bfloat16
        )

    def slots(m, _):
        at = pl.multiple_of(m * 256, 256)
        slot = lax.broadcasted_iota(jnp.int32, (256, 256), 0) + at
        picks = jnp.concatenate(
            [hot(slot == (slots_ref[t : t + 1, :] & 1023)) for t in range(26)], axis=1
        )
        sums = jnp.dot(picks, split[...], preferred_element_type=jnp.float32)
        for side in range(2):
            for block in range(2):
                i = side * 8 + m * 2 + block
                here = pl.ds(pl.multiple_of(i * 128, 128), 128)
                total = sums[128 * block : 128 * block + 128, 128 * side : 128 * side + 128]
                gone = to_column(evict_ref[pl.ds(i, 1), :].astype(jnp.float32))
                cache_ref[here, :] = total * (1.0 - gone)
                sent = total * gone
                upper = poscol[here, :] >> 11
                placed[here, 0:128] = jnp.where(upper == 0, sent, 0.0).astype(jnp.bfloat16)
                placed[here, 128:256] = jnp.where(upper == 1, sent, 0.0).astype(jnp.bfloat16)
        return 0

    lax.fori_loop(0, 4, slots, 0)
    cache_out = pltpu.make_async_copy(cache_ref, cache_hbm, side_sems.at[1])
    cache_out.start()
    whole = pl.ds(32, 4064)
    pltpu.make_async_copy(val.at[whole, :], val.at[whole, :], val_send).wait()

    def send(j, _):
        at = pl.multiple_of(j * 512, 512)
        place = lax.broadcasted_iota(jnp.int32, (512, 128), 0) + at
        picks = jnp.concatenate(
            [hot(place == (pos[i : i + 1, :] & 2047)) for i in range(16)], axis=1
        )
        sums = jnp.dot(picks, placed[...], preferred_element_type=jnp.float32)
        for side in range(2):
            val[pl.ds(pl.multiple_of(at + 2048 * side, 512), 512), :] = sums[
                :, 128 * side : 128 * side + 128
            ].astype(jnp.bfloat16)
            for more in range(2):
                send_blocks(
                    2 * j + more + 8 * side,
                    side == 0 and more == 0,
                    val,
                    rcv,
                    grad_send,
                    lambda c: grad_recv,
                )
        return 0

    lax.fori_loop(0, 4, send, 0)
    rcv[0:32, :] = val[0:32, :]

    for a in (1, 2, 0):
        place, at = room[a]
        for copy in hops[a]:
            copy.wait_recv()

        def gather(j, _):
            sums = weights[place, at + j, 0:64, :].astype(jnp.float32)
            for step in range(3):
                sums = sums + first[a, step, j].astype(jnp.float32)
            second_src[a, :, pl.ds(pl.multiple_of(j * 512, 512), 512)] = sums.astype(jnp.bfloat16)
            return 0

        lax.fori_loop(0, 7, gather, 0)
        for step in (2, 1, 3):
            src = second_src.at[a, pl.ds(16 * step, 16), :]
            hops[a].append(hop(a, 1, step, src, second.at[a, step - 1]))

    pltpu.make_async_copy(rcv.at[whole, :], rcv.at[whole, :], grad_recv).wait()
    for k in range(128):
        g, c = k % 32, k // 32
        half = qcol[32 * k : 32 * k + 32, :] >> 11
        grad = rcv[32 * k : 32 * k + 32, :].astype(jnp.float32)
        at = (g * 4 + c) * 32
        spread[at : at + 32, 0:128] = jnp.where(half == 0, grad, 0.0).astype(jnp.bfloat16)
        spread[at : at + 32, 128:256] = jnp.where(half == 1, grad, 0.0).astype(jnp.bfloat16)
    asked = asked_ref[...]
    asked = jnp.concatenate([asked[32 * c : 32 * c + 32, 0:32] for c in range(4)], axis=1) & 2047

    def update(m, _):
        at = pl.multiple_of(m * 256, 256)
        row = lax.broadcasted_iota(jnp.int32, (256, 128), 0) + at
        picks = jnp.concatenate([hot(row == asked[g : g + 1, :]) for g in range(32)], axis=1)
        sums = jnp.dot(picks, spread[...], preferred_element_type=jnp.float32)
        for side in range(2):
            for block in range(2):
                i = side * 16 + m * 2 + block
                here = pl.ds(pl.multiple_of(i * 128, 128), 128)
                row_grad = sums[128 * block : 128 * block + 128, 128 * side : 128 * side + 128]
                acc = to_column(acc_ref[pl.ds(i, 1), :])
                acc = acc + jnp.sum(row_grad * row_grad, axis=1, keepdims=True) * (1.0 / 128.0)
                new_acc_ref[pl.ds(i, 1), :] = acc.T[0:1, :]
                values = rows_ref[here, :].astype(jnp.float32) * to_column(scale_ref[pl.ds(i, 1), :])
                values = values - LEARN_RATE * row_grad / jnp.sqrt(acc)
                top = jnp.max(jnp.abs(values), axis=1, keepdims=True)
                scale = (jnp.broadcast_to(top, (128, 128)) + 1e-06) / QUANT_TOP
                new_scale_ref[pl.ds(i, 1), :] = scale.T[0:1, :]
                new_rows_ref[here, :] = (values / scale).astype(jnp.bfloat16)
        return 0

    lax.fori_loop(0, 4, update, 0)

    for a in (1, 2, 0):
        for copy in hops[a][3:]:
            copy.wait_recv()
        sums = second_src[a, 0:16, :].astype(jnp.float32)
        for step in range(3):
            sums = sums + second[a, step].astype(jnp.float32)
        for step in range(4):
            piece = sums[4 * step : 4 * step + 4, :]
            third_src[a, step] = jnp.concatenate(
                [piece[:, 896 * i : 896 * i + 896] for i in range(4)], axis=0
            ).astype(jnp.bfloat16)
        for step in (2, 1, 3):
            hops[a].append(hop(a, 2, step, third_src.at[a, step], third.at[a, step - 1]))

    lax.fori_loop(4, 8, update, 0)
    rows_out = pltpu.make_async_copy(new_rows_ref, new_rows_hbm, side_sems.at[2])
    rows_out.start()

    for a, out_ref in enumerate((out_down_ref, out_hid_ref, out_up_ref)):
        for copy in hops[a][6:]:
            copy.wait_recv()
        sums = third_src[a, 0].astype(jnp.float32)
        for step in range(3):
            sums = sums + third[a, step].astype(jnp.float32)
        sums = sums * (1.0 / 128.0)
        sums = jnp.concatenate([sums[4 * i : 4 * i + 4, :] for i in range(4)], axis=1)
        out_ref[...] = sums[:, 0:3341]

    cache_out.wait()
    rows_out.wait()
    for copy in pair + hops[0] + hops[1] + hops[2]:
        copy.wait_send()
    pltpu.make_async_copy(val.at[whole, :], val.at[whole, :], grad_send).wait()


def store_kernel(*refs):
    held, sems = refs[14:21], refs[21]
    inward = [pltpu.make_async_copy(refs[i], held[i], sems.at[0, i]) for i in range(7)]
    outward = [pltpu.make_async_copy(held[i], refs[7 + i], sems.at[1, i]) for i in range(7)]
    for copy in inward:
        copy.start()
    for i in range(7):
        inward[i].wait()
        outward[i].start()
    for copy in outward:
        copy.wait()


def store(*arrays):
    anywhere = pl.BlockSpec(memory_space=pl.ANY)
    return pl.pallas_call(
        store_kernel,
        name="store",
        out_shape=tuple(jax.ShapeDtypeStruct(a.shape, a.dtype) for a in arrays),
        in_specs=[anywhere] * 7,
        out_specs=(anywhere,) * 7,
        scratch_shapes=[pltpu.VMEM(a.shape, a.dtype) for a in arrays]
        + [pltpu.SemaphoreType.DMA((2, 7))],
        compiler_params=pltpu.CompilerParams(vmem_limit_bytes=62 * 2**20),
    )(*arrays)


def train_step(*operands):
    vmem = pl.BlockSpec(memory_space=pltpu.VMEM)
    anywhere = pl.BlockSpec(memory_space=pl.ANY)
    tail = pl.BlockSpec((128, 512), lambda i: (26, 0), memory_space=pltpu.VMEM)
    bf16, f32, i32 = jnp.bfloat16, jnp.float32, jnp.int32
    dense_out = jax.ShapeDtypeStruct((4, 3341), f32)
    dma = pltpu.SemaphoreType.DMA
    return pl.pallas_call(
        step_kernel,
        name="train_step",
        out_shape=(
            jax.ShapeDtypeStruct((4096, 128), bf16),
            jax.ShapeDtypeStruct((32, 128), f32),
            jax.ShapeDtypeStruct((32, 128), f32),
            jax.ShapeDtypeStruct((2048, 128), f32),
            dense_out,
            dense_out,
            dense_out,
        ),
        grid=(1,),
        in_specs=[vmem] * 6 + [anywhere] + [vmem] * 2 + [anywhere] * 3 + [tail] * 3 + [vmem] * 3,
        out_specs=(anywhere, vmem, vmem, anywhere, vmem, vmem, vmem),
        scratch_shapes=[
            pltpu.VMEM((4096, 128), bf16),
            pltpu.VMEM((4096, 128), bf16),
            pltpu.VMEM((2048, 128), f32),
            pltpu.VMEM((3, 14, 256, 512), bf16),
            pltpu.VMEM((1, 3584), f32),
            pltpu.VMEM((128, 1, 128), i32),
            pltpu.VMEM((128, 1, 128), i32),
            pltpu.VMEM((128, 128), i32),
            pltpu.VMEM((4096, 128), bf16),
            pltpu.VMEM((4096, 128), bf16),
            pltpu.VMEM((4096, 128), bf16),
            pltpu.VMEM((1024, 512), bf16),
            pltpu.VMEM((4096, 128), i32),
            pltpu.VMEM((16, 128), i32),
            pltpu.VMEM((2048, 128), i32),
            pltpu.VMEM((2048, 128), f32),
            pltpu.VMEM((1024, 256), bf16),
            pltpu.VMEM((28, 256, 128), f32),
            pltpu.VMEM((3, 256, 3584), bf16),
            pltpu.VMEM((3, 256, 3584), bf16),
            pltpu.VMEM((256, 512), bf16),
            pltpu.VMEM((256, 512), bf16),
            pltpu.VMEM((256, 512), bf16),
            pltpu.VMEM((6656, 256), bf16),
            pltpu.VMEM((2048, 256), bf16),
            pltpu.VMEM((4096, 256), bf16),
            pltpu.VMEM((3, 256, 256), bf16),
            pltpu.VMEM((3, 256, 256), bf16),
            pltpu.VMEM((3, 256, 256), bf16),
            pltpu.VMEM((3, 3, 7, 64, 512), bf16),
            pltpu.VMEM((3, 64, 3584), bf16),
            pltpu.VMEM((3, 3, 16, 3584), bf16),
            pltpu.VMEM((3, 4, 16, 896), bf16),
            pltpu.VMEM((3, 3, 16, 896), bf16),
            dma((3, 13)),
            dma((3,)),
            dma,
            dma,
            dma,
            dma((4,)),
            dma((3, 2)),
            dma((3, 2)),
            dma,
            dma,
            dma((3, 3, 3)),
            dma((3, 3, 3)),
        ],
        compiler_params=pltpu.CompilerParams(
            collective_id=0, has_side_effects=True, vmem_limit_bytes=62 * 2**20
        ),
    )(*operands)


def on_device(
    dense_feats,
    labels,
    slot_ids,
    needed_owner,
    needed_local,
    evicted,
    table_rows,
    table_scale,
    table_acc,
    cross_down,
    cross_up,
    cross_bias,
    hidden_weight,
    hidden_bias,
    out_weight,
):
    up_t = cross_up.T
    results = train_step(
        needed_owner.reshape(1, 2048),
        needed_local.reshape(1, 2048),
        slot_ids.T,
        dense_feats.T,
        labels.reshape(1, 256),
        evicted.reshape(16, 128),
        table_rows,
        table_scale.reshape(32, 128),
        table_acc.reshape(32, 128),
        cross_down,
        up_t,
        hidden_weight,
        cross_down,
        up_t,
        hidden_weight,
        cross_bias,
        hidden_bias.reshape(1, 512),
        out_weight,
    )
    new_rows, new_scale, new_acc, cache, grad_down, grad_hidden, grad_up = store(*results)
    return (
        new_rows,
        new_scale.reshape(4096),
        new_acc.reshape(4096),
        cache,
        grad_down,
        grad_hidden,
        grad_up,
    )


def solution(mesh):
    placed = (
        P(("hst", "chip"), None),
        P(("hst", "chip")),
        P(("hst", "chip"), None),
        P(("hst", "chip"), None),
        P(("hst", "chip")),
        P(("hst", "chip")),
        P(("hst", "chip"), None),
        P(("hst", "chip")),
        P(("hst", "chip")),
        P(),
        P(),
        P(),
        P(),
        P(),
        P(),
    )
    return jax.shard_map(
        on_device,
        mesh=mesh,
        in_specs=placed,
        out_specs=(
            P(("hst", "chip"), None),
            P(("hst", "chip")),
            P(("hst", "chip")),
            P(("hst", "chip"), None),
            P(("hst", "chip"), None),
            P(("hst", "chip"), None),
            P(("hst", "chip"), None),
        ),
        check_vma=False,
    )
```

time: 340 us -> 119 us (0.35)
  waiting for transfers between devices: 124 us -> 0 us
  other arithmetic: 82 us -> 0 us
  Pallas kernels: 48.3 us -> 116 us
  local copies, waits for them, and re-layouts: 28.3 us -> 0 us
  matrix products: 24 us -> 0 us
  starting transfers between devices: 16.8 us -> 0 us
  between operations: 14.5 us -> 0.81 us
    unnamed x2 -> x0, waiting for transfers between devices: 97 us -> none
    pallas_call x1 -> x2, Pallas kernels: 48.3 us -> 116 us  [the longest x1 113 us: train_step(): pl.pallas_call(step_kernel, name='train_step', out_shape=(jax.ShapeDtypeS...]
    scatter-add x2 -> x0, other arithmetic: 61.4 us -> none  [the longest x1 36.5 us: on_device(): jax.ops.segment_sum(emb_grad, slot_ids.reshape(-1), num_segments=need_rows)]
    all_to_all x2 -> x0, waiting for transfers between devices: 27 us -> none  [the longest x1 27 us: send_grads(): lax.all_to_all(outgoing, ('hst', 'chip'), split_axis=0, concat_axis=0, ti...]
    dot_general x10 -> x0, matrix products: 24 us -> none  [the longest x3 12.4 us: contract_first(): lax.dot_general(left, right, (((0,), (0,)), ((), ())), preferred_element_...]
    unnamed x58 -> x0, local copies, waits for them, and re-layouts: 21.8 us -> none
    all_to_all x2 -> x0, starting transfers between devices: 16.7 us -> none  [the longest x1 9.73 us: send_grads(): lax.all_to_all(outgoing, ('hst', 'chip'), split_axis=0, concat_axis=0, ti...]
    unnamed x4 -> x0, other arithmetic: 8.28 us -> none
  transfers between devices with their start and end apart: 3 -> 0, of which waited for: 2 -> 0; matrix products, arithmetic and copies ran while one was open for 29% -> 0% of each run, Pallas kernels for 0% -> 0%
where the time goes in v3:
time: 119 us; the launch traced here: 117 us
  Pallas kernels  116 us (97%)
    pallas_call x1, Pallas kernels, train_step(): pl.pallas_call(step_kernel, name='train_step', out_shape=(jax.ShapeDtypeS...  113 us
    pallas_call x1, Pallas kernels, store(): pl.pallas_call(store_kernel, name='store', out_shape=tuple((jax.ShapeDtyp...  2.71 us

profile of v3, /device:TPU:6, one launch (start us, length us, event | category | flops | bytes accessed | tf_op | source)
XLA Modules:
  0.0 116.7 jit_solution(4747711297091293504)
XLA Ops:
  0.6 113.2 %train_step.1 = (bf16[4096,128]{1,0:T(8,128)(2,1)}, f32[32,128]{1,0:T(8,128)}, f32[32,128]{1,0:T(8,128)}, f32[2048,128]{1,0:T(8,128)}, f32[4,3341]{1,0:T(4,128)}, /*index=5*/f32[4,3341]{1,0:T(4,128)}, f32[4,3341]{1,0:T(4,128)}) custom-call(s32[1,2048]{1,0:T(1,128)} %bitcast.17, s32[1,2048]{1,0:T(1,128)} %bitcast.18, s32[26,256]{1,0:T(8,128)} %bitcast.14, ...), custom_call_target="tpu_custom_call" | custom-call | tf_op jit(solution)/shard_map/train_step/pallas_call | solution.py:683
  113.8 2.7 %store.1 = (bf16[4096,128]{1,0:T(8,128)(2,1)}, f32[32,128]{1,0:T(8,128)}, f32[32,128]{1,0:T(8,128)}, f32[2048,128]{1,0:T(8,128)}, f32[4,3341]{1,0:T(4,128)}, /*index=5*/f32[4,3341]{1,0:T(4,128)}, f32[4,3341]{1,0:T(4,128)}) custom-call(bf16[4096,128]{1,0:T(8,128)(2,1)} %get-tuple-element.21.refs_0_, f32[32,128]{1,0:T(8,128)} %get-tuple-element.22.refs_1_, ...), custom_call_target="tpu_custom_call" | custom-call | tf_op jit(solution)/shard_map/store/pallas_call | solution.py:664

commit v4 on v3

--- a/solution.py
+++ b/solution.py
@@ -79,14 +79,15 @@
     return jnp.concatenate([hot(col == lane + 128 * i) for i in range(count)], axis=1)
 
 
-AXES = (("y", "z", "x"), ("z", "x", "y"), ("x", "y", "z"))
+ORDERS = (("y", "z", "x"), ("z", "x", "y"), ("x", "y", "z"))
+JOBS = ((0, 0, 3, 0), (0, 3, 2, 1), (0, 5, 2, 2), (1, 0, 7, 1), (2, 0, 7, 2))
 DOWN, UP, HID = 0, 1, 2
 
 
-def row_order(array, me):
+def row_order(order, me):
     row = lax.broadcasted_iota(jnp.int32, (512, 512), 0)
     at = {"core": (me["core"] + (row >> 8)) & 1}
-    for stage, axis in enumerate(AXES[array]):
+    for stage, axis in enumerate(ORDERS[order]):
         at[axis] = (me[axis] + (row >> (6 - 2 * stage))) & 3
     source = (at["y"] * 32 + at["z"] * 8 + at["x"] * 2 + at["core"]) * 4 + (row & 3)
     return hot(source == lax.broadcasted_iota(jnp.int32, (512, 512), 1))
@@ -193,11 +194,13 @@
         loads.append(some)
 
     owner = owner_ref[...]
+    far_x = ((owner >> 1) - x) & 3
+    other = (owner - core) & 1
     rel = (
-        (((owner >> 5) - y) & 3) * 32
-        + (((owner >> 3) - z) & 3) * 8
-        + (((owner >> 1) - x) & 3) * 2
-        + ((owner - core) & 1)
+        (((owner >> 5) - y - far_x) & 3) * 32
+        + (((owner >> 3) - z - far_x - 2 * other) & 3) * 8
+        + far_x * 2
+        + other
     )
     sub = lax.broadcasted_iota(jnp.int32, (128, 256), 0)
     upper = hot(
@@ -231,8 +234,13 @@
 
     pl.semaphore_wait(barrier, 127)
 
+    def hosts_of(d):
+        along_y = [((y + d // 4 + i) % 4) * 4 for i in range(4)]
+        along_z = [(z + d % 4 + i) % 4 for i in range(4)]
+        return [along_y[e // 2] + along_z[(e // 2 + 2 * (e % 2)) % 4] for e in range(8)]
+
     def ask(d, _):
-        host = ((y + d // 4) % 4) * 4 + (z + d % 4) % 4
+        hosts = hosts_of(d)
         back = ((4 - d // 4) % 4) * 4 + (4 - d % 4) % 4
         for e in range(8):
 
@@ -242,7 +250,7 @@
                     dst_ref=inc.at[back * 8 + neg_chip(e)],
                     send_sem=req_send,
                     recv_sem=req_recv,
-                    device_id=(host, chips[e]),
+                    device_id=(hosts[e], chips[e]),
                     device_id_type=MESH,
                 ).start()
 
@@ -291,7 +299,7 @@
 
     def send_blocks(d, skip_self, src, dst, send_sem, recv_sem):
         start = pl.multiple_of(d * 256, 256)
-        host = ((y + d // 4) % 4) * 4 + (z + d % 4) % 4
+        hosts = hosts_of(d)
         back = ((4 - d // 4) % 4) * 4 + (4 - d % 4) % 4
         for e in range(8):
 
@@ -301,7 +309,7 @@
                     dst_ref=dst.at[pl.ds(pl.multiple_of(back * 256 + 32 * neg_chip(e), 32), 32), :],
                     send_sem=send_sem,
                     recv_sem=recv_sem(back // 4),
-                    device_id=(host, chips[e]),
+                    device_id=(hosts[e], chips[e]),
                     device_id_type=MESH,
                 ).start()
 
@@ -370,25 +378,25 @@
 
     lax.fori_loop(0, 13, fill, 0)
 
-    def give(array, side, src, dst):
+    def give(slot, src, dst):
         copy = pltpu.make_async_remote_copy(
             src_ref=src,
             dst_ref=dst,
-            send_sem=pair_send.at[array, side],
-            recv_sem=pair_recv.at[array, side],
+            send_sem=pair_send.at[slot],
+            recv_sem=pair_recv.at[slot],
             device_id=partner,
             device_id_type=MESH,
         )
         copy.start()
         return copy
 
-    def ordered(array, values):
-        order = row_order(array, me)
-        mine[array] = contract_last(order[0:256], values).astype(jnp.bfloat16)
-        theirs[array] = contract_last(order[256:512], values).astype(jnp.bfloat16)
-        return give(array, 0, theirs.at[array], lefts.at[array])
-
-    pair = [give(0, 1, base, rights.at[0])]
+    def ordered(job, values):
+        order = row_order(JOBS[job][3], me)
+        mine[job] = contract_last(order[0:256], values).astype(jnp.bfloat16)
+        theirs[job] = contract_last(order[256:512], values).astype(jnp.bfloat16)
+        return give(3 + job, theirs.at[job], lefts.at[job])
+
+    pair = {0: give(0, base, rights.at[0])}
     for copy in loads[DOWN]:
         copy.wait()
     low = jnp.dot(
@@ -408,8 +416,8 @@
         return 0
 
     lax.fori_loop(0, 14, cross, 0)
-    pair.append(give(1, 1, crossed, rights.at[1]))
-    pair.append(ordered(2, low_ref[...]))
+    pair[1] = give(1, crossed, rights.at[1])
+    pair[7] = ordered(4, low_ref[...])
     for copy in loads[HID]:
         copy.wait()
     preact = (
@@ -428,7 +436,7 @@
     grad_hid_ref[...] = (grad_logit * out_w * (sig * (1.0 + preact * (1.0 - sig)))).astype(
         jnp.bfloat16
     )
-    pair.append(ordered(1, grad_hid_ref[...]))
+    pair[6] = ordered(3, grad_hid_ref[...])
 
     def back(j, _):
         cols = pl.ds(pl.multiple_of(j * 256, 256), 256)
@@ -439,51 +447,91 @@
         return 0
 
     lax.fori_loop(0, 14, back, 0)
-    pair.append(give(2, 1, mix, rights.at[2]))
+    pair[2] = give(2, mix, rights.at[2])
     grad_low_ref[...] = jnp.dot(
         mix[...], weights[UP].reshape(3584, 512), preferred_element_type=jnp.float32
     ).astype(jnp.bfloat16)
-    pair.append(ordered(0, grad_low_ref[...]))
+    for job in range(3):
+        pair[3 + job] = ordered(job, grad_low_ref[...])
 
     room = ((UP, 0), (HID, 0), (HID, 7))
 
-    def hop(a, stage, step, src, dst):
+    def hop(job, axis, step, sem, src, dst):
         copy = pltpu.make_async_remote_copy(
             src_ref=src,
             dst_ref=dst,
-            send_sem=sum_send.at[a, stage, step - 1],
-            recv_sem=sum_recv.at[a, stage, step - 1],
-            device_id=shifted(me, AXES[a][stage], step),
+            send_sem=sum_send.at[job, sem],
+            recv_sem=sum_recv.at[job, sem],
+            device_id=shifted(me, axis, step),
             device_id_type=MESH,
         )
         copy.start()
         return copy
 
-    hops = [[], [], []]
-
-    def multiply(a):
+    hops = [[] for _ in JOBS]
+
+    def multiply(job):
+        a, start, count, order = JOBS[job]
+        axis = ORDERS[order][0]
         place, at = room[a]
+        if start == 0:
+            pair[a].wait_recv()
+        pair[3 + job].wait_recv()
 
         def product(j, _):
             cols = pl.ds(pl.multiple_of(j * 512, 512), 512)
-            both = jnp.concatenate([mine[a], lefts[a]], axis=1)
+            both = jnp.concatenate([mine[job], lefts[job]], axis=1)
             wide = jnp.concatenate([wides[a, :, cols], rights[a, :, cols]], axis=0)
             weights[place, at + j] = jnp.dot(both, wide, preferred_element_type=jnp.float32).astype(
                 jnp.bfloat16
             )
             return 0
 
-        lax.fori_loop(0, 7, product, 0)
-        for step in (2, 1, 3):
-            src = weights.at[place, pl.ds(at, 7), pl.ds(64 * step, 64), :]
-            hops[a].append(hop(a, 0, step, src, first.at[a, step - 1]))
-
-    pair[1].wait_recv()
-    pair[3].wait_recv()
-    multiply(1)
-    pair[2].wait_recv()
-    pair[4].wait_recv()
-    multiply(2)
+        lax.fori_loop(start, start + count, product, 0)
+        blocks = pl.ds(at + start, count)
+        to = pl.ds(start, count)
+
+        def rows(first_row):
+            return weights.at[place, blocks, pl.ds(first_row, 32), :]
+
+        upper, lower = pl.ds(0, 32), pl.ds(32, 32)
+        hops[job] = [
+            hop(job, axis, 1, 0, rows(128), first.at[a, 2, to, upper, :]),
+            hop(job, axis, 3, 1, rows(160), first.at[a, 2, to, lower, :]),
+            hop(job, axis, 1, 2, rows(96), first.at[a, 0, to, lower, :]),
+            hop(job, axis, 3, 3, rows(192), first.at[a, 1, to, upper, :]),
+        ]
+
+    def relay(job):
+        a, start, count, order = JOBS[job]
+        axis = ORDERS[order][0]
+        place, at = room[a]
+        blocks = pl.ds(at + start, count)
+        to = pl.ds(start, count)
+        for step, sem, row, part in ((1, 0, 64, 0), (3, 1, 224, 1)):
+            hops[job][sem].wait_recv()
+            side = pl.ds(32 * part, 32)
+
+            def add(j, _):
+                own = weights[place, at + j, row : row + 32, :].astype(jnp.float32)
+                came = first[a, 2, j, 32 * part : 32 * part + 32, :].astype(jnp.float32)
+                weights[place, at + j, row : row + 32, :] = (own + came).astype(jnp.bfloat16)
+                return 0
+
+            lax.fori_loop(start, start + count, add, 0)
+            hops[job].append(
+                hop(
+                    job,
+                    axis,
+                    step,
+                    4 + part,
+                    weights.at[place, blocks, pl.ds(row, 32), :],
+                    first.at[a, part, to, side, :],
+                )
+            )
+
+    multiply(3)
+    multiply(4)
 
     def last(j, _):
         grad = contract_last(grad_low_ref[...], weights[DOWN, j])
@@ -495,9 +543,10 @@
         return 0
 
     lax.fori_loop(0, 13, last, 0)
-    pair[0].wait_recv()
-    pair[5].wait_recv()
-    multiply(0)
+    relay(3)
+    for job in range(3):
+        multiply(job)
+    relay(4)
     ids = jnp.concatenate([slots_ref[...], jnp.zeros((102, 256), jnp.int32)], axis=0).T
     for t in range(26):
         half = jnp.broadcast_to(ids[:, t : t + 1] >> 10, (256, 128))
@@ -530,6 +579,8 @@
         return 0
 
     lax.fori_loop(0, 4, slots, 0)
+    for job in range(3):
+        relay(job)
     cache_out = pltpu.make_async_copy(cache_ref, cache_hbm, side_sems.at[1])
     cache_out.start()
     whole = pl.ds(32, 4064)
@@ -560,22 +611,25 @@
     lax.fori_loop(0, 4, send, 0)
     rcv[0:32, :] = val[0:32, :]
 
-    for a in (1, 2, 0):
+    for job in (3, 4, 0, 1, 2):
+        a, start, count, order = JOBS[job]
         place, at = room[a]
-        for copy in hops[a]:
+        for copy in hops[job][2:6]:
             copy.wait_recv()
 
         def gather(j, _):
             sums = weights[place, at + j, 0:64, :].astype(jnp.float32)
-            for step in range(3):
-                sums = sums + first[a, step, j].astype(jnp.float32)
+            for side in range(2):
+                sums = sums + first[a, side, j].astype(jnp.float32)
             second_src[a, :, pl.ds(pl.multiple_of(j * 512, 512), 512)] = sums.astype(jnp.bfloat16)
             return 0
 
-        lax.fori_loop(0, 7, gather, 0)
+        lax.fori_loop(start, start + count, gather, 0)
+        cols = pl.ds(start * 512, count * 512)
         for step in (2, 1, 3):
-            src = second_src.at[a, pl.ds(16 * step, 16), :]
-            hops[a].append(hop(a, 1, step, src, second.at[a, step - 1]))
+            src = second_src.at[a, pl.ds(16 * step, 16), cols]
+            dst = second.at[a, step - 1, :, cols]
+            hops[job].append(hop(job, ORDERS[order][1], step, 5 + step, src, dst))
 
     pltpu.make_async_copy(rcv.at[whole, :], rcv.at[whole, :], grad_recv).wait()
     for k in range(128):
@@ -611,37 +665,47 @@
 
     lax.fori_loop(0, 4, update, 0)
 
-    for a in (1, 2, 0):
-        for copy in hops[a][3:]:
+    for job in (3, 4, 0, 1, 2):
+        a, start, count, order = JOBS[job]
+        cols = slice(start * 512, (start + count) * 512)
+        wide = count * 128
+        for copy in hops[job][6:]:
             copy.wait_recv()
-        sums = second_src[a, 0:16, :].astype(jnp.float32)
+        sums = second_src[a, 0:16, cols].astype(jnp.float32)
         for step in range(3):
-            sums = sums + second[a, step].astype(jnp.float32)
+            sums = sums + second[a, step, :, cols].astype(jnp.float32)
         for step in range(4):
             piece = sums[4 * step : 4 * step + 4, :]
-            third_src[a, step] = jnp.concatenate(
-                [piece[:, 896 * i : 896 * i + 896] for i in range(4)], axis=0
+            third_src[a, step, :, start * 128 : start * 128 + wide] = jnp.concatenate(
+                [piece[:, wide * i : wide * i + wide] for i in range(4)], axis=0
             ).astype(jnp.bfloat16)
+        narrow = pl.ds(start * 128, wide)
         for step in (2, 1, 3):
-            hops[a].append(hop(a, 2, step, third_src.at[a, step], third.at[a, step - 1]))
+            src = third_src.at[a, step, :, narrow]
+            dst = third.at[a, step - 1, :, narrow]
+            hops[job].append(hop(job, ORDERS[order][2], step, 8 + step, src, dst))
 
     lax.fori_loop(4, 8, update, 0)
     rows_out = pltpu.make_async_copy(new_rows_ref, new_rows_hbm, side_sems.at[2])
     rows_out.start()
 
-    for a, out_ref in enumerate((out_down_ref, out_hid_ref, out_up_ref)):
-        for copy in hops[a][6:]:
+    out_refs = (out_down_ref, out_hid_ref, out_up_ref)
+    for job in (3, 4, 0, 1, 2):
+        a, start, count, order = JOBS[job]
+        for copy in hops[job][9:]:
             copy.wait_recv()
-        sums = third_src[a, 0].astype(jnp.float32)
+        cols = slice(start * 128, (start + count) * 128)
+        sums = third_src[a, 0, :, cols].astype(jnp.float32)
         for step in range(3):
-            sums = sums + third[a, step].astype(jnp.float32)
+            sums = sums + third[a, step, :, cols].astype(jnp.float32)
         sums = sums * (1.0 / 128.0)
         sums = jnp.concatenate([sums[4 * i : 4 * i + 4, :] for i in range(4)], axis=1)
-        out_ref[...] = sums[:, 0:3341]
+        end = min(3341, (start + count) * 512)
+        out_refs[a][:, start * 512 : end] = sums[:, 0 : end - start * 512]
 
     cache_out.wait()
     rows_out.wait()
-    for copy in pair + hops[0] + hops[1] + hops[2]:
+    for copy in list(pair.values()) + [copy for some in hops for copy in some]:
         copy.wait_send()
     pltpu.make_async_copy(val.at[whole, :], val.at[whole, :], grad_send).wait()
 
@@ -722,9 +786,9 @@
             pltpu.VMEM((6656, 256), bf16),
             pltpu.VMEM((2048, 256), bf16),
             pltpu.VMEM((4096, 256), bf16),
-            pltpu.VMEM((3, 256, 256), bf16),
-            pltpu.VMEM((3, 256, 256), bf16),
-            pltpu.VMEM((3, 256, 256), bf16),
+            pltpu.VMEM((5, 256, 256), bf16),
+            pltpu.VMEM((5, 256, 256), bf16),
+            pltpu.VMEM((5, 256, 256), bf16),
             pltpu.VMEM((3, 3, 7, 64, 512), bf16),
             pltpu.VMEM((3, 64, 3584), bf16),
             pltpu.VMEM((3, 3, 16, 3584), bf16),
@@ -736,12 +800,12 @@
             dma,
             dma,
             dma((4,)),
-            dma((3, 2)),
-            dma((3, 2)),
+            dma((8,)),
+            dma((8,)),
             dma,
             dma,
-            dma((3, 3, 3)),
-            dma((3, 3, 3)),
+            dma((5, 12)),
+            dma((5, 12)),
         ],
         compiler_params=pltpu.CompilerParams(
             collective_id=0, has_side_effects=True, vmem_limit_bytes=62 * 2**20

time: 119 us -> 115 us (0.966); the launches traced: 117 us -> 115 us
  Pallas kernels: 116 us -> 114 us
    pallas_call x1, Pallas kernels: 113 us -> 112 us  [train_step(): pl.pallas_call(step_kernel, name='train_step', out_shape=(jax.ShapeDtypeS...]
where the time goes in v4:
time: 115 us
  Pallas kernels  114 us (99%)
    pallas_call x1, Pallas kernels, train_step(): pl.pallas_call(step_kernel, name='train_step', out_shape=(jax.ShapeDtypeS...  112 us
    pallas_call x1, Pallas kernels, store(): pl.pallas_call(store_kernel, name='store', out_shape=tuple((jax.ShapeDtyp...  2.71 us

profile of v4, /device:TPU:6, one launch (start us, length us, event | category | flops | bytes accessed | tf_op | source)
XLA Modules:
  0.0 115.1 jit_solution(6943138201860577010)
XLA Ops:
  0.6 111.6 %train_step.1 = (bf16[4096,128]{1,0:T(8,128)(2,1)}, f32[32,128]{1,0:T(8,128)}, f32[32,128]{1,0:T(8,128)}, f32[2048,128]{1,0:T(8,128)}, f32[4,3341]{1,0:T(4,128)}, /*index=5*/f32[4,3341]{1,0:T(4,128)}, f32[4,3341]{1,0:T(4,128)}) custom-call(s32[1,2048]{1,0:T(1,128)} %bitcast.17, s32[1,2048]{1,0:T(1,128)} %bitcast.18, s32[26,256]{1,0:T(8,128)} %bitcast.14, ...), custom_call_target="tpu_custom_call" | custom-call | tf_op jit(solution)/shard_map/train_step/pallas_call | solution.py:747
  112.2 2.7 %store.1 = (bf16[4096,128]{1,0:T(8,128)(2,1)}, f32[32,128]{1,0:T(8,128)}, f32[32,128]{1,0:T(8,128)}, f32[2048,128]{1,0:T(8,128)}, f32[4,3341]{1,0:T(4,128)}, /*index=5*/f32[4,3341]{1,0:T(4,128)}, f32[4,3341]{1,0:T(4,128)}) custom-call(bf16[4096,128]{1,0:T(8,128)(2,1)} %get-tuple-element.21.refs_0_, f32[32,128]{1,0:T(8,128)} %get-tuple-element.22.refs_1_, ...), custom_call_target="tpu_custom_call" | custom-call | tf_op jit(solution)/shard_map/store/pallas_call | solution.py:728

commit v5 on v4

--- a/solution.py
+++ b/solution.py
@@ -604,7 +604,7 @@
                     val,
                     rcv,
                     grad_send,
-                    lambda c: grad_recv,
+                    lambda c: grad_recv.at[c],
                 )
         return 0
 
@@ -631,27 +631,68 @@
             dst = second.at[a, step - 1, :, cols]
             hops[job].append(hop(job, ORDERS[order][1], step, 5 + step, src, dst))
 
-    pltpu.make_async_copy(rcv.at[whole, :], rcv.at[whole, :], grad_recv).wait()
-    for k in range(128):
-        g, c = k % 32, k // 32
-        half = qcol[32 * k : 32 * k + 32, :] >> 11
-        grad = rcv[32 * k : 32 * k + 32, :].astype(jnp.float32)
-        at = (g * 4 + c) * 32
-        spread[at : at + 32, 0:128] = jnp.where(half == 0, grad, 0.0).astype(jnp.bfloat16)
-        spread[at : at + 32, 128:256] = jnp.where(half == 1, grad, 0.0).astype(jnp.bfloat16)
     asked = asked_ref[...]
-    asked = jnp.concatenate([asked[32 * c : 32 * c + 32, 0:32] for c in range(4)], axis=1) & 2047
+    wanted = [
+        jnp.concatenate(
+            [asked[32 * c + 8 * i : 32 * c + 8 * i + 8, 0:32] for i in range(4)], axis=1
+        )
+        & 2047
+        for c in range(4)
+    ]
+    arrival = (0, 2, 3, 1)
+
+    def arrange(nth):
+        c = arrival[nth]
+        if c == 0:
+            landed = rcv.at[pl.ds(32, 992), :]
+        else:
+            landed = rcv.at[pl.ds(1024 * c, 1024), :]
+        pltpu.make_async_copy(landed, landed, grad_recv.at[c]).wait()
+        for i in range(32):
+            k = 32 * c + i
+            half = qcol[32 * k : 32 * k + 32, :] >> 11
+            grad = rcv[32 * k : 32 * k + 32, :].astype(jnp.float32)
+            at = 1024 * nth + ((i % 8) * 4 + i // 8) * 32
+            spread[at : at + 32, 0:128] = jnp.where(half == 0, grad, 0.0).astype(jnp.bfloat16)
+            spread[at : at + 32, 128:256] = jnp.where(half == 1, grad, 0.0).astype(jnp.bfloat16)
+
+    def row_sums(m, first_nth):
+        row = lax.broadcasted_iota(jnp.int32, (256, 128), 0) + pl.multiple_of(m * 256, 256)
+        picks = jnp.concatenate(
+            [
+                hot(row == wanted[arrival[nth]][g : g + 1, :])
+                for nth in (first_nth, first_nth + 1)
+                for g in range(8)
+            ],
+            axis=1,
+        )
+        return jnp.dot(
+            picks,
+            spread[1024 * first_nth : 1024 * first_nth + 2048, :],
+            preferred_element_type=jnp.float32,
+        )
+
+    def early(m, _):
+        sums = row_sums(m, 0)
+        factor[2 * m] = sums[:, 0:128]
+        factor[2 * m + 1] = sums[:, 128:256]
+        return 0
+
+    arrange(0)
+    arrange(1)
+    lax.fori_loop(0, 8, early, 0)
+    arrange(2)
+    arrange(3)
 
     def update(m, _):
-        at = pl.multiple_of(m * 256, 256)
-        row = lax.broadcasted_iota(jnp.int32, (256, 128), 0) + at
-        picks = jnp.concatenate([hot(row == asked[g : g + 1, :]) for g in range(32)], axis=1)
-        sums = jnp.dot(picks, spread[...], preferred_element_type=jnp.float32)
+        sums = row_sums(m, 2)
         for side in range(2):
+            before = factor[2 * m + side]
             for block in range(2):
                 i = side * 16 + m * 2 + block
                 here = pl.ds(pl.multiple_of(i * 128, 128), 128)
                 row_grad = sums[128 * block : 128 * block + 128, 128 * side : 128 * side + 128]
+                row_grad = row_grad + before[128 * block : 128 * block + 128]
                 acc = to_column(acc_ref[pl.ds(i, 1), :])
                 acc = acc + jnp.sum(row_grad * row_grad, axis=1, keepdims=True) * (1.0 / 128.0)
                 new_acc_ref[pl.ds(i, 1), :] = acc.T[0:1, :]
@@ -803,7 +844,7 @@
             dma((8,)),
             dma((8,)),
             dma,
-            dma,
+            dma((4,)),
             dma((5, 12)),
             dma((5, 12)),
         ],

time: 115 us -> 113 us (0.983)
  Pallas kernels: 114 us -> 112 us
    pallas_call x1, Pallas kernels: 112 us -> 110 us  [train_step(): pl.pallas_call(step_kernel, name='train_step', out_shape=(jax.ShapeDtypeS...]
where the time goes in v5:
time: 113 us
  Pallas kernels  112 us (99%)
    pallas_call x1, Pallas kernels, train_step(): pl.pallas_call(step_kernel, name='train_step', out_shape=(jax.ShapeDtypeS...  110 us
    pallas_call x1, Pallas kernels, store(): pl.pallas_call(store_kernel, name='store', out_shape=tuple((jax.ShapeDtyp...  2.71 us

profile of v5, /device:TPU:6, one launch (start us, length us, event | category | flops | bytes accessed | tf_op | source)
XLA Modules:
  0.0 113.1 jit_solution(13569769867027290158)
XLA Ops:
  0.6 109.6 %train_step.1 = (bf16[4096,128]{1,0:T(8,128)(2,1)}, f32[32,128]{1,0:T(8,128)}, f32[32,128]{1,0:T(8,128)}, f32[2048,128]{1,0:T(8,128)}, f32[4,3341]{1,0:T(4,128)}, /*index=5*/f32[4,3341]{1,0:T(4,128)}, f32[4,3341]{1,0:T(4,128)}) custom-call(s32[1,2048]{1,0:T(1,128)} %bitcast.17, s32[1,2048]{1,0:T(1,128)} %bitcast.18, s32[26,256]{1,0:T(8,128)} %bitcast.14, ...), custom_call_target="tpu_custom_call" | custom-call | tf_op jit(solution)/shard_map/train_step/pallas_call | solution.py:788
  110.3 2.7 %store.1 = (bf16[4096,128]{1,0:T(8,128)(2,1)}, f32[32,128]{1,0:T(8,128)}, f32[32,128]{1,0:T(8,128)}, f32[2048,128]{1,0:T(8,128)}, f32[4,3341]{1,0:T(4,128)}, /*index=5*/f32[4,3341]{1,0:T(4,128)}, f32[4,3341]{1,0:T(4,128)}) custom-call(bf16[4096,128]{1,0:T(8,128)(2,1)} %get-tuple-element.21.refs_0_, f32[32,128]{1,0:T(8,128)} %get-tuple-element.22.refs_1_, ...), custom_call_target="tpu_custom_call" | custom-call | tf_op jit(solution)/shard_map/store/pallas_call | solution.py:769
